TPU v7x, 512 devices: a whole 4x4x16 slice. The times are simulated.
512 devices in a mesh: space: 64 (over x_lo, z, core), probe: 8 (over x_hi, y).
Axes of the slice: x: 4 (x_hi: 2, x_lo: 2; x = x_hi * 2 + x_lo), y: 4, z: 16, core: 2. Of those that a mesh axis runs over, the one named last changes fastest.
Arguments:
- site_class: int32 [10, 192, 2, 128], P(None, 'space'), may hold values from 0 to 127, as said below
- probe_signs: int32 [30, 32, 192, 2, 128], P(None, 'probe', 'space'), may hold values from 0 to 1
- masses: float32 [128], replicated, may hold values from 1 to 4
- force_blocks: float32 [27, 30, 30], replicated, may hold values from -0.018 to 0.518, as said below
Outputs:
- moments: float32 [4, 128], replicated
- last_term: float32 [30, 32, 192, 2, 128], P(None, 'probe', 'space')
Inputs may be any that keep to these rules, and one draw needn't show every extreme that they name: `site_class`: an atom in a cell with first index x has a class in the window of 4 classes that starts at (x // 3) * 2, taken modulo 128. force_blocks[26 - o] is the transpose of force_blocks[o] for every offset index o.
All inputs are finite; a program needn't handle non-finite values.
Results may differ from a plain program's by a relative error of at most 0.00012.
Values sent between devices are 32-bit elements; how exact they have to be, the bound alone decides.
No kernel may reach another device: no remote copies, remote signals or barrier semaphores. Data moves between devices by JAX's collectives and lax.ppermute only.
A program may use at most 64 MiB of HBM per device.

v0:
```python
import jax
import jax.numpy as jnp
from jax import lax
from jax.sharding import PartitionSpec as P

exact_mode = lax.Precision.HIGHEST


def extended(cells, sides, width):
    for axis, dim in sides:
        count = lax.axis_size(axis)
        head = lax.slice_in_dim(cells, 0, width, axis=dim)
        tail = lax.slice_in_dim(cells, cells.shape[dim] - width, cells.shape[dim], axis=dim)
        cells = jnp.concatenate(
            [
                lax.ppermute(tail, axis, [(i, (i + 1) % count) for i in range(count)]),
                cells,
                lax.ppermute(head, axis, [((i + 1) % count, i) for i in range(count)]),
            ],
            axis=dim,
        )
    return cells


def stencil_apply(padded, force_blocks):
    extent = padded.shape[2] - 2
    accumulated = jnp.zeros(padded.shape[:2] + (extent,) + padded.shape[3:], jnp.float32)
    for column in range(9):
        shift_x = column // 3 - 1
        shift_y = column % 3 - 1
        base = lax.slice_in_dim(padded, 1 + shift_x, 1 + shift_x + extent, axis=2)
        base = jnp.roll(base, -shift_y, axis=3)
        stacked = jnp.concatenate(
            [jnp.roll(base, 1, axis=4), base, jnp.roll(base, -1, axis=4)], axis=0
        )
        joined = jnp.concatenate(
            [force_blocks[3 * column], force_blocks[3 * column + 1], force_blocks[3 * column + 2]],
            axis=1,
        )
        accumulated = accumulated + jnp.einsum(
            "ab,bpxyz->apxyz", joined, stacked, precision=exact_mode
        )
    return accumulated


def class_onehot(labels, nclass):
    return (labels[:, None] == jnp.arange(nclass, dtype=jnp.int32)[None, :]).astype(jnp.float32)


def atom_scales(site_class, masses):
    inv_root = 1.0 / jnp.sqrt(masses)
    class_rows = site_class.reshape(site_class.shape[0], -1)

    def lookup(labels):
        return jnp.dot(class_onehot(labels, masses.shape[0]), inv_root, precision=exact_mode)

    return lax.map(lookup, class_rows).reshape(site_class.shape)


def class_sums(product, site_class, nclass):
    atom_count = site_class.shape[0]
    per_atom = product.reshape(atom_count, 3, product.shape[1], -1).sum(axis=(1, 2))
    labels = site_class.reshape(atom_count, -1)

    def one_atom(atom_pair):
        return jnp.dot(atom_pair[0], class_onehot(atom_pair[1], nclass), precision=exact_mode)

    return jnp.sum(lax.map(one_atom, (per_atom, labels)), axis=0)


def global_moment(product, site_class, nclass):
    return lax.psum(class_sums(product, site_class, nclass), ("space", "probe"))


def body(site_class, probe_signs, masses, force_blocks):
    nclass = masses.shape[0]
    first_term = (2 * probe_signs - 1).astype(jnp.float32)
    atom_scale = atom_scales(site_class, masses)
    comp_scale = jnp.repeat(atom_scale, 3, axis=0)[:, None]

    def operator_apply(field):
        weighted = comp_scale * field
        padded = extended(weighted, (("space", 2),), 1)
        return comp_scale * stencil_apply(padded, force_blocks)

    second_term = operator_apply(first_term)
    third_term = 2.0 * operator_apply(second_term) - first_term
    last_term = 2.0 * operator_apply(third_term) - second_term
    products = (
        first_term * first_term,
        first_term * second_term,
        first_term * third_term,
        first_term * last_term,
    )
    sums = jnp.stack([global_moment(term_product, site_class, nclass) for term_product in products])
    probes_all = first_term.shape[1] * lax.axis_size("probe")
    class_stride = nclass // lax.axis_size("space")
    scale = 1.0 / (
        probes_all
        * first_term.shape[0]
        * first_term.shape[2]
        * first_term.shape[3]
        * first_term.shape[4]
        / class_stride
    )
    return (sums * scale, last_term)


def solution(mesh):
    return jax.shard_map(
        body,
        mesh=mesh,
        in_specs=(P(None, "space", None, None), P(None, "probe", "space", None, None), P(), P()),
        out_specs=(P(), P(None, "probe", "space", None, None)),
        check_vma=False,
    )
```

profile of v0, /device:TPU:1, one launch (start us, length us, event | category | flops | bytes accessed | tf_op | source)
XLA Modules:
  0.0 201.6 jit_solution(1709832285658495043)
XLA Ops:
  0.6 0.8 reshape.33
  1.4 0.7 sqrt.3
  2.1 5.0 %while.51 = (s32[]{:T(128)}, f32[10,768]{1,0:T(8,128)S(1)}, s32[10,768]{1,0:T(8,128)S(1)}, f32[128]{0:T(128)S(1)}, s32[]{:T(128)}, /*index=5*/s32[]{:T(128)}) while((s32[]{:T(128)}, f32[10,768]{1,0:T(8,128)S(1)}, s32[10,768]{1,0:T(8,128)S(1)}, f32[128]{0:T(128)S(1)}, s32[]{:T(128)}, /*index=5*/s32[]{:T(128)}) %tuple.176), condition=%wide.region_7.8_spmd, body=%wide.region_6.7_spmd.sunk | while | flops 1277954 | bytes 19029 | solution.py:57
  2.1 0.4 fusion.291
  2.6 0.4 fusion.291
  3.1 0.4 fusion.291
  3.6 0.4 fusion.291
  4.1 0.4 fusion.291
  4.6 0.4 fusion.291
  5.1 0.4 fusion.291
  5.6 0.4 fusion.291
  6.1 0.4 fusion.291
  6.6 0.4 fusion.291
  7.3 8.9 %collective-permute-start.1 = (f32[30,4,1,2,128]{4,0,3,2,1:T(8,128)S(1)}, f32[30,4,1,2,128]{4,0,3,2,1:T(8,128)S(1)}, u32[]{:S(2)}, u32[]{:S(2)}) collective-permute-start(f32[30,4,1,2,128]{4,0,3,2,1:T(8,128)S(1)} %get-tuple-element.284), channel_id=1, source_target_pairs={{8,0},{16,8},{24,16},{32,24},{40,32},{48,40},{56,48},{64,56},{72,6... | collective-permute-start | bytes 368648 | tf_op jit(solution)/shard_map/ppermute | solution.py:18
  16.2 1.9 collective-permute-start
  18.7 4.8 %collective-permute-done = f32[30,4,1,2,128]{4,0,3,2,1:T(8,128)S(1)} collective-permute-done((f32[30,4,1,2,128]{4,0,3,2,1:T(8,128)S(1)}, f32[30,4,1,2,128]{4,0,3,2,1:T(8,128)S(1)}, u32[]{:S(2)}, u32[]{:S(2)}) %collective-permute-start) | collective-permute-done | bytes 122912 | tf_op jit(solution)/shard_map/ppermute | solution.py:16
  24.5 1.0 fusion.213
  25.5 0.4 fusion.180
  26.0 0.4 fusion.179
  26.4 1.0 convolution_add_fusion.23
  27.4 1.0 convolution_add_fusion.22
  28.4 1.0 convolution_add_fusion.21
  29.3 1.0 convolution_add_fusion.20
  30.3 1.0 convolution_add_fusion.19
  31.3 1.0 convolution_add_fusion.18
  32.3 1.0 convolution_add_fusion.17
  33.2 1.0 broadcast_multiply_fusion.1
  34.2 7.6 %collective-permute-start.3 = (f32[30,4,1,2,128]{4,0,3,2,1:T(8,128)S(1)}, f32[30,4,1,2,128]{4,0,3,2,1:T(8,128)S(1)}, u32[]{:S(2)}, u32[]{:S(2)}) collective-permute-start(f32[30,4,1,2,128]{4,0,3,2,1:T(8,128)S(1)} %get-tuple-element.262), channel_id=1, source_target_pairs={{8,0},{16,8},{24,16},{32,24},{40,32},{48,40},{56,48},{64,56},{72,6... | collective-permute-start | bytes 368648 | tf_op jit(solution)/shard_map/ppermute | solution.py:18
  41.8 2.1 %collective-permute-start.2 = (f32[30,4,1,2,128]{4,0,3,2,1:T(8,128)S(1)}, f32[30,4,1,2,128]{4,0,3,2,1:T(8,128)S(1)}, u32[]{:S(2)}, u32[]{:S(2)}) collective-permute-start(f32[30,4,1,2,128]{4,0,3,2,1:T(8,128)S(1)} %get-tuple-element.263), channel_id=1, source_target_pairs={{0,8},{8,16},{16,24},{24,32},{32,40},{40,48},{48,56},{56,64},{64,7... | collective-permute-start | bytes 368648 | tf_op jit(solution)/shard_map/ppermute | solution.py:16
  43.9 1.7 collective-permute-done.2
  46.9 1.0 fusion.216
  47.9 0.4 fusion.172
  48.4 0.4 fusion.171
  48.8 1.0 convolution_add_fusion.15
  49.7 1.0 convolution_add_fusion.14
  50.7 1.0 convolution_add_fusion.13
  51.7 1.0 convolution_add_fusion.12
  52.7 1.0 convolution_add_fusion.11
  53.6 1.0 convolution_add_fusion.10
  54.6 1.0 convolution_add_fusion.9
  55.6 1.0 broadcast_multiply_fusion
  56.6 6.5 %collective-permute-start.5 = (f32[30,4,1,2,128]{4,0,3,2,1:T(8,128)S(1)}, f32[30,4,1,2,128]{4,0,3,2,1:T(8,128)S(1)}, u32[]{:S(2)}, u32[]{:S(2)}) collective-permute-start(f32[30,4,1,2,128]{4,0,3,2,1:T(8,128)S(1)} %get-tuple-element.240), channel_id=1, source_target_pairs={{8,0},{16,8},{24,16},{32,24},{40,32},{48,40},{56,48},{64,56},{72,6... | collective-permute-start | bytes 368648 | tf_op jit(solution)/shard_map/ppermute | solution.py:18
  63.1 2.1 %collective-permute-start.4 = (f32[30,4,1,2,128]{4,0,3,2,1:T(8,128)S(1)}, f32[30,4,1,2,128]{4,0,3,2,1:T(8,128)S(1)}, u32[]{:S(2)}, u32[]{:S(2)}) collective-permute-start(f32[30,4,1,2,128]{4,0,3,2,1:T(8,128)S(1)} %get-tuple-element.241), channel_id=1, source_target_pairs={{0,8},{8,16},{16,24},{24,32},{32,40},{40,48},{48,56},{56,64},{64,7... | collective-permute-start | bytes 368648 | tf_op jit(solution)/shard_map/ppermute | solution.py:16
  65.3 1.7 collective-permute-done.4
  68.2 1.0 fusion.219
  69.2 0.4 fusion.164
  69.7 0.4 fusion.163
  70.0 1.0 convolution_add_fusion.7
  71.0 1.0 convolution_add_fusion.6
  72.0 1.0 convolution_add_fusion.5
  73.0 1.0 convolution_add_fusion.4
  73.9 1.0 convolution_add_fusion.3
  74.9 1.0 convolution_add_fusion.2
  75.9 1.0 convolution_add_fusion.1
  76.9 1.2 multiply_reduce_fusion.3
  78.3 4.4 %while.54 = (s32[]{:T(128)}, f32[10,128]{1,0:T(8,128)S(1)}, f32[10,768]{1,0:T(8,128)S(1)}, s32[10,768]{1,0:T(8,128)S(1)}, s32[]{:T(128)}, /*index=5*/s32[]{:T(128)}) while((s32[]{:T(128)}, f32[10,128]{1,0:T(8,128)S(1)}, f32[10,768]{1,0:T(8,128)S(1)}, s32[10,768]{1,0:T(8,128)S(1)}, s32[]{:T(128)}, /*index=5*/s32[]{:T(128)}) %tuple.191), condition=%wide.region_23.24_spmd, body=%wide.region_22.23_spmd.sunk | while | flops 1277954 | bytes 14937 | solution.py:68
  79.4 0.3 fusion.297
  80.7 0.3 fusion.297
  83.0 4.1 %while.53 = (s32[]{:T(128)}, f32[10,128]{1,0:T(8,128)S(1)}, f32[10,768]{1,0:T(8,128)S(1)}, s32[10,768]{1,0:T(8,128)S(1)}, s32[]{:T(128)}, /*index=5*/s32[]{:T(128)}) while((s32[]{:T(128)}, f32[10,128]{1,0:T(8,128)S(1)}, f32[10,768]{1,0:T(8,128)S(1)}, s32[10,768]{1,0:T(8,128)S(1)}, s32[]{:T(128)}, /*index=5*/s32[]{:T(128)}) %tuple.192), condition=%wide.region_17.18_spmd, body=%wide.region_16.17_spmd.sunk | while | flops 1277954 | bytes 14937 | solution.py:68
  87.4 4.1 %while.52 = (s32[]{:T(128)}, f32[10,128]{1,0:T(8,128)S(1)}, f32[10,768]{1,0:T(8,128)S(1)}, s32[10,768]{1,0:T(8,128)S(1)}, s32[]{:T(128)}, /*index=5*/s32[]{:T(128)}) while((s32[]{:T(128)}, f32[10,128]{1,0:T(8,128)S(1)}, f32[10,768]{1,0:T(8,128)S(1)}, s32[10,768]{1,0:T(8,128)S(1)}, s32[]{:T(128)}, /*index=5*/s32[]{:T(128)}) %tuple.193), condition=%wide.region_11.12_spmd, body=%wide.region_10.11_spmd.sunk | while | flops 1277954 | bytes 14937 | solution.py:68
  91.8 4.1 %while.50 = (s32[]{:T(128)}, f32[10,128]{1,0:T(8,128)S(1)}, f32[10,768]{1,0:T(8,128)S(1)}, s32[10,768]{1,0:T(8,128)S(1)}, s32[]{:T(128)}, /*index=5*/s32[]{:T(128)}) while((s32[]{:T(128)}, f32[10,128]{1,0:T(8,128)S(1)}, f32[10,768]{1,0:T(8,128)S(1)}, s32[10,768]{1,0:T(8,128)S(1)}, s32[]{:T(128)}, /*index=5*/s32[]{:T(128)}) %tuple.194), condition=%wide.region_3.4_spmd, body=%wide.region_2.3_spmd.sunk | while | flops 1277954 | bytes 14937 | solution.py:68
  95.9 1.0 copy.21
  97.0 104.1 %all-reduce = (f32[1,128]{1,0:T(1,128)S(1)}, f32[1,128]{1,0:T(1,128)S(1)}, f32[1,128]{1,0:T(1,128)S(1)}, f32[1,128]{1,0:T(1,128)S(1)}) all-reduce(f32[1,128]{1,0:T(1,128)S(1)} %bitcast.152, f32[1,128]{1,0:T(1,128)S(1)} %bitcast.153, f32[1,128]{1,0:T(1,128)S(1)} %bitcast.154, ...), channel_id=1, replica_groups=mesh['space'=64,'probe'=8] {'space','probe'}, use_global_device_ids=true, to_apply=%region_25.26 | all-reduce | flops 512 | bytes 4096 | tf_op jit(solution)/shard_map/psum | solution.py:72
  201.1 0.6 maximum_multiply_fusion
  (202 shorter events, 21.0 us)
Async XLA Ops:
  2.1 5.1 %copy-start.1 = (s32[30,4,3,2,128]{4,3,2,1,0:T(2,128)S(1)}, s32[30,4,3,2,128]{4,3,2,1,0:T(2,128)}, u32[]{:S(2)}) copy-start(s32[30,4,3,2,128]{4,3,2,1,0:T(2,128)} %param.15) | copy-start | bytes 1105924
  7.3 10.9 %copy-start = (f32[27,30,30]{2,1,0:T(8,128)S(1)}, f32[27,30,30]{2,1,0:T(8,128)}, u32[]{:S(2)}) copy-start(f32[27,30,30]{2,1,0:T(8,128)} %param.17) | copy-start | bytes 291604
  7.3 11.4 %collective-permute-start.1 = (f32[30,4,1,2,128]{4,0,3,2,1:T(8,128)S(1)}, f32[30,4,1,2,128]{4,0,3,2,1:T(8,128)S(1)}, u32[]{:S(2)}, u32[]{:S(2)}) collective-permute-start(f32[30,4,1,2,128]{4,0,3,2,1:T(8,128)S(1)} %get-tuple-element.284), channel_id=1, source_target_pairs={{8,0},{16,8},{24,16},{32,24},{40,32},{48,40},{56,48},{64,56},{72,6... | collective-permute-start | bytes 368648 | tf_op jit(solution)/shard_map/ppermute | solution.py:18
  16.2 7.2 %collective-permute-start = (f32[30,4,1,2,128]{4,0,3,2,1:T(8,128)S(1)}, f32[30,4,1,2,128]{4,0,3,2,1:T(8,128)S(1)}, u32[]{:S(2)}, u32[]{:S(2)}) collective-permute-start(f32[30,4,1,2,128]{4,0,3,2,1:T(8,128)S(1)} %get-tuple-element.285), channel_id=1, source_target_pairs={{0,8},{8,16},{16,24},{24,32},{32,40},{40,48},{48,56},{56,64},{64,7... | collective-permute-start | bytes 368648 | tf_op jit(solution)/shard_map/ppermute | solution.py:16
  34.2 9.7 %collective-permute-start.3 = (f32[30,4,1,2,128]{4,0,3,2,1:T(8,128)S(1)}, f32[30,4,1,2,128]{4,0,3,2,1:T(8,128)S(1)}, u32[]{:S(2)}, u32[]{:S(2)}) collective-permute-start(f32[30,4,1,2,128]{4,0,3,2,1:T(8,128)S(1)} %get-tuple-element.262), channel_id=1, source_target_pairs={{8,0},{16,8},{24,16},{32,24},{40,32},{48,40},{56,48},{64,56},{72,6... | collective-permute-start | bytes 368648 | tf_op jit(solution)/shard_map/ppermute | solution.py:18
  41.8 3.9 %collective-permute-start.2 = (f32[30,4,1,2,128]{4,0,3,2,1:T(8,128)S(1)}, f32[30,4,1,2,128]{4,0,3,2,1:T(8,128)S(1)}, u32[]{:S(2)}, u32[]{:S(2)}) collective-permute-start(f32[30,4,1,2,128]{4,0,3,2,1:T(8,128)S(1)} %get-tuple-element.263), channel_id=1, source_target_pairs={{0,8},{8,16},{16,24},{24,32},{32,40},{40,48},{48,56},{56,64},{64,7... | collective-permute-start | bytes 368648 | tf_op jit(solution)/shard_map/ppermute | solution.py:16
  56.6 8.6 %collective-permute-start.5 = (f32[30,4,1,2,128]{4,0,3,2,1:T(8,128)S(1)}, f32[30,4,1,2,128]{4,0,3,2,1:T(8,128)S(1)}, u32[]{:S(2)}, u32[]{:S(2)}) collective-permute-start(f32[30,4,1,2,128]{4,0,3,2,1:T(8,128)S(1)} %get-tuple-element.240), channel_id=1, source_target_pairs={{8,0},{16,8},{24,16},{32,24},{40,32},{48,40},{56,48},{64,56},{72,6... | collective-permute-start | bytes 368648 | tf_op jit(solution)/shard_map/ppermute | solution.py:18
  63.1 3.9 %collective-permute-start.4 = (f32[30,4,1,2,128]{4,0,3,2,1:T(8,128)S(1)}, f32[30,4,1,2,128]{4,0,3,2,1:T(8,128)S(1)}, u32[]{:S(2)}, u32[]{:S(2)}) collective-permute-start(f32[30,4,1,2,128]{4,0,3,2,1:T(8,128)S(1)} %get-tuple-element.241), channel_id=1, source_target_pairs={{0,8},{8,16},{16,24},{24,32},{32,40},{40,48},{48,56},{56,64},{64,7... | collective-permute-start | bytes 368648 | tf_op jit(solution)/shard_map/ppermute | solution.py:16
where the time goes:
time: 202 us
  blocking collectives  104 us (51%)
  matrix products  43.1 us (21%)
  starting transfers between devices  29.1 us (14%)
  waiting for transfers between devices  8.23 us (4%)
  other arithmetic  7.57 us (4%)
  local copies, waits for them, and re-layouts  6.56 us (3%)
    psum x1, blocking collectives, global_moment(): return lax.psum(class_sums(product, site_class, nclass), ('space', 'probe'))  104 us
    dot_general x27, matrix products, stencil_apply(): jnp.einsum('ab,bpxyz->apxyz', joined, stacked, precision=exact_mode)  26.4 us
    ppermute x3, starting transfers between devices, extended(): lax.ppermute(head, axis, [((i + 1) % count, i) for i in range(count)])  22.9 us
    dot_general x40, matrix products, one_atom(): jnp.dot(atom_pair[0], class_onehot(atom_pair[1], nclass), precision=exact...  13 us
    ppermute x3, waiting for transfers between devices, extended(): lax.ppermute(tail, axis, [(i, (i + 1) % count) for i in range(count)])  8.22 us
    ppermute x3, starting transfers between devices, extended(): lax.ppermute(tail, axis, [(i, (i + 1) % count) for i in range(count)])  6.16 us
  transfers between devices with their start and end apart: 6, of which 3 were waited for; matrix products, arithmetic and copies ran while one was open for 0% of the time, Pallas kernels for 0%

commit v1 on v0

v1 whole, which is shorter than its diff:
```python
import jax
import jax.numpy as jnp
from jax import lax
from jax.experimental import pallas as pl
from jax.experimental.pallas import tpu as pltpu
from jax.sharding import Mesh, PartitionSpec as P

SPACE = ("xl", "z", "core")
PROBE = ("xh", "y")
NEAR = ("xl", "core", "xh", "y")

COMP, PAD = 30, 32
ATOMS, ATOM_PAD = 10, 16
NP, CX, NY, NZ = 4, 3, 2, 128
PLANES = 3 * CX
ROWS = NY * PAD
WIDE = NP * NZ
SIGN_ROWS = CX * NY * NP * PAD
PAY_ROWS = SIGN_ROWS + CX * NY * ATOM_PAD
WIN = 4


def weight_kernel(fb_ref, hi_ref, lo_ref, full):
    full[...] = jnp.zeros_like(full)
    for dx in range(3):
        for dz in range(3):
            same = fb_ref[9 * dx + 3 + dz]
            other = fb_ref[9 * dx + dz] + fb_ref[9 * dx + 6 + dz]
            for y in range(NY):
                for y2 in range(NY):
                    r, c = dz * ROWS + y * PAD, dx * ROWS + y2 * PAD
                    full[r : r + COMP, c : c + COMP] = same if y == y2 else other
    hi = full[...].astype(jnp.bfloat16)
    hi_ref[...] = hi
    lo_ref[...] = (full[...] - hi.astype(jnp.float32)).astype(jnp.bfloat16)


def main_kernel(mass_ref, own_ref, a_ref, b_ref, wh_ref, wl_ref, out_ref, pm_ref, uh, ul, v0s, v1s, ss, rels):
    core = lax.axis_index("core")
    idx = (lax.axis_index("xl") * lax.axis_size("z") + lax.axis_index("z")) * 2 + core
    is_even = core == 0

    def rows(slab, start, count):
        where = slice(start, start + count)
        if slab == 1:
            return own_ref[where, :]
        near, far = a_ref[where, :], b_ref[where, :]
        return jnp.where(is_even, far, near) if slab == 0 else jnp.where(is_even, near, far)

    spread = (
        lax.broadcasted_iota(jnp.int32, (PAD, ATOM_PAD), 0) // 3
        == lax.broadcasted_iota(jnp.int32, (PAD, ATOM_PAD), 1)
    ).astype(jnp.bfloat16)
    valid = lax.broadcasted_iota(jnp.int32, (PAD, NZ), 0) < COMP

    for slab in range(3):
        base = 2 * ((idx + slab - 1) & 63)
        inv = [1.0 / jnp.sqrt(jnp.full((1, NZ), mass_ref[(base + j) & 127], jnp.float32)) for j in range(WIN)]
        labels = jnp.concatenate(
            [rows(slab, SIGN_ROWS + i * ATOM_PAD, ATOM_PAD) for i in range(CX * NY)], axis=1
        )
        labels = jnp.dot(spread, labels.astype(jnp.float32).astype(jnp.bfloat16), preferred_element_type=jnp.float32)
        rel = (labels.astype(jnp.int32) - base) & 127
        for x in range(CX):
            for y in range(NY):
                i = x * NY + y
                part = rel[:, i * NZ : (i + 1) * NZ]
                scale = jnp.where(part == 0, inv[0], jnp.where(part == 1, inv[1], jnp.where(part == 2, inv[2], inv[3])))
                scale = jnp.where(valid, scale, 0.0)
                at = (slab * CX + x) * ROWS + y * PAD
                ss[at : at + PAD, :] = scale
                if slab == 1:
                    rels[i * PAD : (i + 1) * PAD, :] = jnp.where(valid, part, -1)
                for p in range(NP):
                    sign = rows(slab, (i * NP + p) * PAD, PAD)
                    v0 = (2 * sign - 1).astype(jnp.float32)
                    lanes = slice(p * NZ, (p + 1) * NZ)
                    v0s[at : at + PAD, lanes] = v0
                    u = scale * v0
                    hi = u.astype(jnp.bfloat16)
                    uh[0, at : at + PAD, lanes] = hi
                    ul[0, at : at + PAD, lanes] = (u - hi.astype(jnp.float32)).astype(jnp.bfloat16)

    wh, wl = wh_ref[...], wl_ref[...]
    sums = [[jnp.zeros((8, NZ), jnp.float32) for _ in range(WIN)] for _ in range(4)]

    def add_moments(n, plane, total):
        for j in range(WIN):
            mask = rels[(plane - CX) * ROWS : (plane - CX + 1) * ROWS, :] == j
            picked = jnp.where(mask, total, 0.0)
            sums[n][j] = sums[n][j] + sum(picked[8 * k : 8 * k + 8] for k in range(ROWS // 8))

    for step in range(3):
        for plane in range(step + 1, PLANES - 1 - step):
            here = slice(plane * ROWS, (plane + 1) * ROWS)
            around = slice((plane - 1) * ROWS, (plane + 2) * ROWS)
            scale = ss[here, :]
            inner = CX <= plane < 2 * CX
            total = jnp.zeros((ROWS, NZ), jnp.float32)
            if inner and step == 0:
                count = sum(v0s[here, p * NZ : (p + 1) * NZ] * v0s[here, p * NZ : (p + 1) * NZ] for p in range(NP))
                add_moments(0, plane, count)
            for pair in range(NP // 2):
                wide = slice(pair * 2 * NZ, (pair + 1) * 2 * NZ)
                high, low = uh[step, around, wide], ul[step, around, wide]
                t = (
                    jnp.dot(wh, high, preferred_element_type=jnp.float32)
                    + jnp.dot(wh, low, preferred_element_type=jnp.float32)
                    + jnp.dot(wl, high, preferred_element_type=jnp.float32)
                )
                for q in range(2):
                    lanes = slice((pair * 2 + q) * NZ, (pair * 2 + q + 1) * NZ)
                    col = slice(q * NZ, (q + 1) * NZ)
                    g = (
                        pltpu.roll(t[0:ROWS, col], 1, 1)
                        + t[ROWS : 2 * ROWS, col]
                        + pltpu.roll(t[2 * ROWS :, col], NZ - 1, 1)
                    ) * scale
                    v0 = v0s[here, lanes]
                    if step == 0:
                        v = g
                        v1s[here, lanes] = v
                    elif step == 1:
                        v = 2.0 * g - v0
                    else:
                        v = 2.0 * g - v1s[here, lanes]
                        out_ref[plane - CX, :, lanes] = v
                    if step < 2:
                        u = scale * v
                        hi = u.astype(jnp.bfloat16)
                        uh[step + 1, here, lanes] = hi
                        ul[step + 1, here, lanes] = (u - hi.astype(jnp.float32)).astype(jnp.bfloat16)
                    if inner:
                        total = total + v0 * v
            if inner:
                add_moments(step + 1, plane, total)

    lane = lax.broadcasted_iota(jnp.int32, (4, NZ), 1)
    moments = jnp.zeros((4, NZ), jnp.float32)
    for j in range(WIN):
        stacked = jnp.concatenate([jnp.sum(sums[n][j], axis=0, keepdims=True) for n in range(4)], axis=0)
        value = jnp.sum(stacked, axis=1, keepdims=True)
        moments = moments + jnp.where(lane == ((2 * idx + j) & 127), value, 0.0)
    pm_ref[...] = jnp.broadcast_to(moments[None], pm_ref.shape)


VMEM = pl.BlockSpec(memory_space=pltpu.VMEM)
SMEM = pl.BlockSpec(memory_space=pltpu.SMEM)


def body(site_class, probe_signs, masses, force_blocks):
    signs = jnp.transpose(probe_signs, (2, 3, 1, 0, 4))
    signs = jnp.pad(signs, ((0, 0),) * 3 + ((0, PAD - COMP), (0, 0))).reshape(SIGN_ROWS, NZ)
    labels = jnp.transpose(site_class, (1, 2, 0, 3))
    labels = jnp.pad(labels, ((0, 0),) * 2 + ((0, ATOM_PAD - ATOMS), (0, 0))).reshape(-1, NZ)
    payload = jnp.concatenate([signs, labels], axis=0)

    count = 64
    far = lax.ppermute(payload, SPACE, [(i, (i + 1) % count if i % 2 else (i - 1) % count) for i in range(count)])
    near = lax.ppermute(payload, SPACE, [(i, i ^ 1) for i in range(count)])

    wide = 3 * ROWS
    high, low = pl.pallas_call(
        weight_kernel,
        out_shape=(jax.ShapeDtypeStruct((wide, wide), jnp.bfloat16),) * 2,
        in_specs=[VMEM],
        out_specs=(VMEM, VMEM),
        scratch_shapes=[pltpu.VMEM((wide, wide), jnp.float32)],
        cost_estimate=pl.CostEstimate(flops=1000000, bytes_accessed=300000, transcendentals=0),
        name="weights",
    )(force_blocks)

    group = 32
    last, parts = pl.pallas_call(
        main_kernel,
        out_shape=(
            jax.ShapeDtypeStruct((CX, ROWS, WIDE), jnp.float32),
            jax.ShapeDtypeStruct((group, 4, NZ), jnp.float32),
        ),
        in_specs=[SMEM] + [VMEM] * 5,
        out_specs=(VMEM, VMEM),
        scratch_shapes=[
            pltpu.VMEM((3, PLANES * ROWS, WIDE), jnp.bfloat16),
            pltpu.VMEM((3, PLANES * ROWS, WIDE), jnp.bfloat16),
            pltpu.VMEM((PLANES * ROWS, WIDE), jnp.float32),
            pltpu.VMEM((PLANES * ROWS, WIDE), jnp.float32),
            pltpu.VMEM((PLANES * ROWS, NZ), jnp.float32),
            pltpu.VMEM((CX * ROWS, NZ), jnp.int32),
        ],
        compiler_params=pltpu.CompilerParams(vmem_limit_bytes=40 * 2**20),
        cost_estimate=pl.CostEstimate(flops=2000000000, bytes_accessed=2000000, transcendentals=0),
        name="chebyshev",
    )(masses, payload, near, far, high, low)

    parts = lax.all_to_all(parts, NEAR, 0, 0, tiled=True).sum(0)
    parts = jnp.broadcast_to(parts[None], (lax.axis_size("z"), 4, NZ))
    moments = lax.all_to_all(parts, "z", 0, 0, tiled=True).sum(0) * (1.0 / 368640)

    last = last.reshape(CX, NY, PAD, NP, NZ)[:, :, :COMP]
    return moments, jnp.transpose(last, (2, 3, 0, 1, 4))


def solution(mesh):
    fine = Mesh(mesh.devices.reshape(2, 16, 2, 2, 4), SPACE + PROBE)
    return jax.shard_map(
        body,
        mesh=fine,
        in_specs=(P(None, SPACE, None, None), P(None, PROBE, SPACE, None, None), P(), P()),
        out_specs=(P(), P(None, PROBE, SPACE, None, None)),
        check_vma=False,
    )
```

time: 202 us -> 63.1 us (0.31)
  blocking collectives: 104 us -> 15.9 us
  matrix products: 43.1 us -> 0 us
  other arithmetic: 7.57 us -> 0.68 us
  starting transfers between devices: 29.1 us -> 23.5 us
  Pallas kernels: 0 us -> 5.51 us
  waiting for transfers between devices: 8.23 us -> 10.4 us
    psum x1 -> x0, blocking collectives: 104 us -> none  [global_moment(): return lax.psum(class_sums(product, site_class, nclass), ('space', 'probe'))]
    dot_general x77 -> x0, matrix products: 43.1 us -> none  [the longest x27 26.4 us: stencil_apply(): jnp.einsum('ab,bpxyz->apxyz', joined, stacked, precision=exact_mode)]
    all_to_all x0 -> x1, blocking collectives: none -> 15.9 us  [body(): parts = lax.all_to_all(parts, NEAR, 0, 0, tiled=True).sum(0)]
    ppermute x6 -> x2, starting transfers between devices: 29.1 us -> 15.2 us  [the longest x1 10.2 us: body(): near = lax.ppermute(payload, SPACE, [(i, i ^ 1) for i in range(count)])]
    all_to_all x0 -> x1, waiting for transfers between devices: none -> 10.4 us  [body(): lax.all_to_all(parts, 'z', 0, 0, tiled=True).sum(0) * (1.0 / 368640)]
    all_to_all x0 -> x1, starting transfers between devices: none -> 8.29 us  [body(): lax.all_to_all(parts, 'z', 0, 0, tiled=True).sum(0) * (1.0 / 368640)]
    ppermute x6 -> x2, waiting for transfers between devices: 8.23 us -> 0.01 us  [the longest x1 0.01 us: body(): lax.ppermute(payload, SPACE, [(i, (i + 1) % count if i % 2 else (i - 1) %...]
    concatenate x33 -> x1, other arithmetic: 6.5 us -> 0.03 us  [body(): payload = jnp.concatenate([signs, labels], axis=0)]
  transfers between devices with their start and end apart: 6 -> 3, of which waited for: 3 -> 1; matrix products, arithmetic and copies ran while one was open for 0% -> 2% of each run, Pallas kernels for 0% -> 3%
where the time goes in v1:
time: 63.1 us; the launch traced here: 62.6 us
  starting transfers between devices  23.5 us (37%)
  blocking collectives  15.9 us (25%)
  waiting for transfers between devices  10.4 us (16%)
  local copies, waits for them, and re-layouts  5.99 us (9%)
  Pallas kernels  5.51 us (9%)
  between operations  0.72 us (1%)
  other arithmetic  0.68 us (1%)
    all_to_all x1, blocking collectives, body(): parts = lax.all_to_all(parts, NEAR, 0, 0, tiled=True).sum(0)  15.9 us
    all_to_all x1, waiting for transfers between devices, body(): lax.all_to_all(parts, 'z', 0, 0, tiled=True).sum(0) * (1.0 / 368640)  10.4 us
    ppermute x1, starting transfers between devices, body(): near = lax.ppermute(payload, SPACE, [(i, i ^ 1) for i in range(count)])  10.2 us
    all_to_all x1, starting transfers between devices, body(): lax.all_to_all(parts, 'z', 0, 0, tiled=True).sum(0) * (1.0 / 368640)  8.29 us
    unnamed x9, local copies, waits for them, and re-layouts  5.19 us
    ppermute x1, starting transfers between devices, body(): lax.ppermute(payload, SPACE, [(i, (i + 1) % count if i % 2 else (i - 1) %...  4.94 us
    pallas_call x1, Pallas kernels, body(): pl.pallas_call(main_kernel, out_shape=(jax.ShapeDtypeStruct((CX, ROWS, WI...  3.64 us
    pallas_call x1, Pallas kernels, body(): pl.pallas_call(weight_kernel, out_shape=(jax.ShapeDtypeStruct((wide, wide...  1.87 us
  transfers between devices with their start and end apart: 3, of which 1 were waited for; matrix products, arithmetic and copies ran while one was open for 2% of the time, Pallas kernels for 3%

profile of v1, /device:TPU:1, one launch (start us, length us, event | category | flops | bytes accessed | tf_op | source)
XLA Modules:
  0.0 62.6 jit_solution(16507643996512470314)
XLA Ops:
  0.6 0.8 %copy.19 = s32[3,2,10,128]{3,2,1,0:T(8,128)S(1)} copy(s32[3,2,10,128]{3,1,0,2:T(2,128)} %bitcast.11) | data formatting | bytes 61440
  1.4 1.1 %copy.18 = s32[3,2,4,30,128]{4,3,2,1,0:T(8,128)S(1)} copy(s32[3,2,4,30,128]{4,1,0,2,3:T(2,128)} %bitcast.8) | data formatting | bytes 737280
  2.5 4.9 %collective-permute-start.1 = (s32[864,128]{1,0:T(8,128)S(1)}, s32[864,128]{1,0:T(8,128)S(1)}, u32[]{:S(2)}, u32[]{:S(2)}) collective-permute-start(s32[864,128]{1,0:T(8,128)S(1)} %pad_add_fusion.own_ref), channel_id=1, source_target_pairs={{0,504},{8,16},{16,8},{24,32},{32,24},{40,48},{48,40},{56,64},{64,... | collective-permute-start | bytes 1327112 | tf_op jit(solution)/shard_map/ppermute | solution.py:159
  7.5 10.2 %collective-permute-start = (s32[864,128]{1,0:T(8,128)S(1)}, s32[864,128]{1,0:T(8,128)S(1)}, u32[]{:S(2)}, u32[]{:S(2)}) collective-permute-start(s32[864,128]{1,0:T(8,128)S(1)} %pad_add_fusion.own_ref), channel_id=1, source_target_pairs={{0,8},{8,0},{16,24},{24,16},{32,40},{40,32},{48,56},{56,48},{64,72... | collective-permute-start | bytes 1327112 | tf_op jit(solution)/shard_map/ppermute | solution.py:160
  17.7 1.9 %weights.1 = (bf16[192,192]{1,0:T(8,128)(2,1)}, bf16[192,192]{1,0:T(8,128)(2,1)}) custom-call(f32[27,30,30]{2,1,0:T(8,128)} %fb_ref.1), custom_call_target="tpu_custom_call" | custom-call | flops 1000000 | bytes 300000 | tf_op jit(solution)/shard_map/weights/pallas_call | solution.py:163
  19.6 0.0 collective-permute-done.1.b_ref
  19.6 0.0 collective-permute-done.a_ref
  19.6 0.0 copy-start.2
  19.6 0.7 %copy-done.2 = f32[128]{0:T(128)S(1)} copy-done((f32[128]{0:T(128)S(1)}, f32[128]{0:T(128)}, u32[]{:S(2)}) %copy-start.2) | copy-done | bytes 536
  20.3 0.0 copy-start
  20.3 0.9 %copy-done = bf16[192,192]{1,0:T(8,128)(2,1)S(1)} copy-done((bf16[192,192]{1,0:T(8,128)(2,1)S(1)}, bf16[192,192]{1,0:T(8,128)(2,1)}, u32[]{:S(2)}) %copy-start) | copy-done | bytes 73752
  21.2 0.0 copy-start.1
  21.2 0.9 %copy-done.1 = bf16[192,192]{1,0:T(8,128)(2,1)S(1)} copy-done((bf16[192,192]{1,0:T(8,128)(2,1)S(1)}, bf16[192,192]{1,0:T(8,128)(2,1)}, u32[]{:S(2)}) %copy-start.1) | copy-done | bytes 73752
  22.1 3.6 %chebyshev.1 = (f32[3,64,512]{2,1,0:T(8,128)S(1)}, f32[32,4,128]{2,1,0:T(4,128)S(1)}) custom-call(f32[128]{0:T(128)S(1)} %copy-done.2, s32[864,128]{1,0:T(8,128)S(1)} %pad_add_fusion.own_ref, s32[864,128]{1,0:T(8,128)S(1)} %collective-permute-done.a_ref, s32[864,128]{1,0:T(8,128)S(1)} %collective-permute-done.1.b_ref, bf16[192,192]{1,0:T(8,128)(2,1)S(1)} %copy-done, ...), custom_call_target="tpu_custom_call" | custom-call | flops 2000000000 | bytes 2000000 | tf_op jit(solution)/shard_map/chebyshev/pallas_call | solution.py:174
  25.7 15.9 %all_to_all.10 = f32[32,4,128]{2,1,0:T(4,128)S(1)} all-to-all(f32[32,4,128]{2,1,0:T(4,128)S(1)} %get-tuple-element.8), channel_id=1, replica_groups=mesh['xl'=2,'z'=16,'core'=2,'xh'=2,'y'=4] {'xl','core','xh','y'}, dimensions={0} | all-to-all | bytes 131072 | tf_op jit(solution)/shard_map/all_to_all | solution.py:195
  41.6 0.6 broadcast_in_dim.2
  42.2 8.3 %all-to-all-start.1 = ((f32[16,4,128]{2,1,0:T(4,128)}), f32[16,4,128]{2,1,0:T(4,128)S(1)}, u32[]{:S(2)}, u32[]{:S(2)}) async-start(f32[16,4,128]{2,1,0:T(4,128)} %broadcast_in_dim.2), calls=%async_computation.1 | async-start | bytes 65536 | tf_op jit(solution)/shard_map/all_to_all | solution.py:197
  50.5 0.1 reshape.16
  50.7 0.9 %copy.21 = f32[3,2,30,4,128]{4,1,0,3,2:T(2,128)} copy(f32[3,2,30,4,128]{4,3,2,1,0:T(4,128)S(1)} %slice.4) | data formatting | bytes 737280
  51.6 10.4 %all-to-all-done.1 = f32[16,4,128]{2,1,0:T(4,128)S(1)} async-done(((f32[16,4,128]{2,1,0:T(4,128)}), f32[16,4,128]{2,1,0:T(4,128)S(1)}, u32[]{:S(2)}, u32[]{:S(2)}) %all-to-all-start.1) | async-done | bytes 32800 | tf_op jit(solution)/shard_map/all_to_all | solution.py:197
  62.0 0.6 broadcast_multiply_fusion
  (6 shorter events, 0.2 us)
Async XLA Ops:
  2.5 17.1 %collective-permute-start.1 = (s32[864,128]{1,0:T(8,128)S(1)}, s32[864,128]{1,0:T(8,128)S(1)}, u32[]{:S(2)}, u32[]{:S(2)}) collective-permute-start(s32[864,128]{1,0:T(8,128)S(1)} %pad_add_fusion.own_ref), channel_id=1, source_target_pairs={{0,504},{8,16},{16,8},{24,32},{32,24},{40,48},{48,40},{56,64},{64,... | collective-permute-start | bytes 1327112 | tf_op jit(solution)/shard_map/ppermute | solution.py:159
  7.5 12.1 %collective-permute-start = (s32[864,128]{1,0:T(8,128)S(1)}, s32[864,128]{1,0:T(8,128)S(1)}, u32[]{:S(2)}, u32[]{:S(2)}) collective-permute-start(s32[864,128]{1,0:T(8,128)S(1)} %pad_add_fusion.own_ref), channel_id=1, source_target_pairs={{0,8},{8,0},{16,24},{24,16},{32,40},{40,32},{48,56},{56,48},{64,72... | collective-permute-start | bytes 1327112 | tf_op jit(solution)/shard_map/ppermute | solution.py:160
  19.6 0.7 %copy-start.2 = (f32[128]{0:T(128)S(1)}, f32[128]{0:T(128)}, u32[]{:S(2)}) copy-start(f32[128]{0:T(128)} %mass_ref.1) | copy-start | bytes 1540
  20.3 0.9 %copy-start = (bf16[192,192]{1,0:T(8,128)(2,1)S(1)}, bf16[192,192]{1,0:T(8,128)(2,1)}, u32[]{:S(2)}) copy-start(bf16[192,192]{1,0:T(8,128)(2,1)} %get-tuple-element.6.wh_ref) | copy-start | bytes 221188
  21.2 0.9 %copy-start.1 = (bf16[192,192]{1,0:T(8,128)(2,1)S(1)}, bf16[192,192]{1,0:T(8,128)(2,1)}, u32[]{:S(2)}) copy-start(bf16[192,192]{1,0:T(8,128)(2,1)} %get-tuple-element.7.wl_ref) | copy-start | bytes 221188
  42.2 19.8 %all-to-all-start.1 = ((f32[16,4,128]{2,1,0:T(4,128)}), f32[16,4,128]{2,1,0:T(4,128)S(1)}, u32[]{:S(2)}, u32[]{:S(2)}) async-start(f32[16,4,128]{2,1,0:T(4,128)} %broadcast_in_dim.2), calls=%async_computation.1 | async-start | bytes 65536 | tf_op jit(solution)/shard_map/all_to_all | solution.py:197

commit v2 on v1

v2 whole, which is shorter than its diff:
```python
import jax
import jax.numpy as jnp
from jax import lax
from jax.experimental import pallas as pl
from jax.experimental.pallas import tpu as pltpu
from jax.sharding import Mesh, PartitionSpec as P

SPACE = ("xl", "z", "core")
PROBE = ("xh", "y")
NEAR = ("xl", "core", "xh", "y")

COMP, PAD = 30, 32
ATOMS, ATOM_PAD = 10, 16
NP, CX, NY, NZ = 4, 3, 2, 128
PLANES = 3 * CX
ROWS = NY * PAD
WIDE = NP * NZ
CELLS = CX * NY
SIGN_ROWS = COMP * NP * CELLS
LABEL_ROWS = ATOMS * CELLS
PAY_ROWS = SIGN_ROWS + LABEL_ROWS
WIN = 4


def split(u):
    hi = u.astype(jnp.bfloat16)
    return hi, (u - hi.astype(jnp.float32)).astype(jnp.bfloat16)


def window_of(idx):
    return 2 * (idx & 63)


def own_index():
    return (lax.axis_index("xl") * lax.axis_size("z") + lax.axis_index("z")) * 2 + lax.axis_index("core")


def load_slab(rows, base, inv, emit):
    spread = (
        lax.broadcasted_iota(jnp.int32, (PAD, ATOM_PAD), 0) // 3
        == lax.broadcasted_iota(jnp.int32, (PAD, ATOM_PAD), 1)
    ).astype(jnp.bfloat16)
    valid = lax.broadcasted_iota(jnp.int32, (PAD, NZ), 0) < COMP
    labels = jnp.concatenate([rows(pl.ds(SIGN_ROWS + i, ATOMS, stride=CELLS)) for i in range(CELLS)], axis=1)
    labels = jnp.concatenate([labels, jnp.zeros((ATOM_PAD - ATOMS, CELLS * NZ), jnp.int32)], axis=0)
    labels = jnp.dot(spread, labels.astype(jnp.float32).astype(jnp.bfloat16), preferred_element_type=jnp.float32)
    rel = (labels.astype(jnp.int32) - base) & 127
    for i in range(CX * NY):
        part = rel[:, i * NZ : (i + 1) * NZ]
        scale = jnp.where(part == 0, inv[0], jnp.where(part == 1, inv[1], jnp.where(part == 2, inv[2], inv[3])))
        scale = jnp.where(valid, scale, 0.0)
        signs = []
        for p in range(NP):
            sign = rows(pl.ds(p * CELLS + i, COMP, stride=NP * CELLS))
            sign = jnp.concatenate([sign, jnp.zeros((PAD - COMP, NZ), jnp.int32)], axis=0)
            signs.append((2 * sign - 1).astype(jnp.float32))
        emit(slice(i * PAD, (i + 1) * PAD), scale, jnp.where(valid, part, -1), signs)


def payload_kernel(signs_ref, labels_ref, pay_ref, sems):
    copies = [
        pltpu.make_async_copy(signs_ref.reshape(SIGN_ROWS, NZ), pay_ref.at[0:SIGN_ROWS, :], sems.at[0]),
        pltpu.make_async_copy(labels_ref.reshape(LABEL_ROWS, NZ), pay_ref.at[SIGN_ROWS : SIGN_ROWS + LABEL_ROWS, :], sems.at[1]),
    ]
    for copy in copies:
        copy.start()
    for copy in copies:
        copy.wait()


def prepare_kernel(mass_ref, fb_ref, own_ref, w_ref, inv_ref, uh_ref, ul_ref, v0_ref, s_ref, rel_ref, full):
    full[...] = jnp.zeros_like(full)
    for dx in range(3):
        for dz in range(3):
            same = fb_ref[9 * dx + 3 + dz]
            other = fb_ref[9 * dx + dz] + fb_ref[9 * dx + 6 + dz]
            for y in range(NY):
                for y2 in range(NY):
                    r, c = dz * ROWS + y * PAD, dx * ROWS + y2 * PAD
                    full[r : r + COMP, c : c + COMP] = same if y == y2 else other
    w_ref[0 : 3 * ROWS, :], w_ref[3 * ROWS :, :] = split(full[...])

    idx = own_index()
    inv = []
    for slab in range(3):
        base = window_of(idx + slab - 1)
        row = [1.0 / jnp.sqrt(jnp.full((1, NZ), mass_ref[(base + j) & 127], jnp.float32)) for j in range(WIN)]
        inv.append(row)
        if slab != 1:
            for j in range(WIN):
                at = slab * 2 + j
                inv_ref[at : at + 1, :] = row[j]

    def emit(at, scale, rel, signs):
        s_ref[at, :] = scale
        rel_ref[at, :] = rel
        for p, v0 in enumerate(signs):
            lanes = slice(p * NZ, (p + 1) * NZ)
            v0_ref[at, lanes] = v0
            uh_ref[at, lanes], ul_ref[at, lanes] = split(scale * v0)

    load_slab(lambda at: own_ref[at, :], window_of(idx), inv[1], emit)


def main_kernel(
    a_ref, b_ref, w_ref, inv_ref, uh_ref, ul_ref, v0_ref, s_ref, rel_ref, out_ref, pm_ref, uh, ul, v0s, v1s, ss, result, sem
):
    idx = own_index()
    is_even = lax.axis_index("core") == 0
    own = slice(CX * ROWS, 2 * CX * ROWS)
    uh[0, own, :] = uh_ref[...]
    ul[0, own, :] = ul_ref[...]

    for slab in (0, 2):

        def rows(at, slab=slab):
            near, far = a_ref[at, :], b_ref[at, :]
            return jnp.where(is_even, far, near) if slab == 0 else jnp.where(is_even, near, far)

        def emit(at, scale, rel, signs, slab=slab):
            at = slice(at.start + slab * CX * ROWS, at.stop + slab * CX * ROWS)
            ss[at, :] = scale
            for p, v0 in enumerate(signs):
                lanes = slice(p * NZ, (p + 1) * NZ)
                v0s[at, lanes] = v0
                uh[0, at, lanes], ul[0, at, lanes] = split(scale * v0)

        inv = [inv_ref[slab * 2 + j : slab * 2 + j + 1, :] for j in range(WIN)]
        load_slab(rows, window_of(idx + slab - 1), inv, emit)

    weights = w_ref[...]
    high_weights = w_ref[0 : 3 * ROWS, :]
    sums = [[jnp.zeros((8, NZ), jnp.float32) for _ in range(WIN)] for _ in range(4)]

    def add_moments(n, inner, total):
        for j in range(WIN):
            picked = jnp.where(rel_ref[inner, :] == j, total, 0.0)
            sums[n][j] = sums[n][j] + sum(picked[8 * k : 8 * k + 8] for k in range(ROWS // 8))

    writes = []
    for step in range(3):
        for plane in range(step + 1, PLANES - 1 - step):
            here = slice(plane * ROWS, (plane + 1) * ROWS)
            around = slice((plane - 1) * ROWS, (plane + 2) * ROWS)
            is_own = CX <= plane < 2 * CX
            inner = slice((plane - CX) * ROWS, (plane - CX + 1) * ROWS)
            scale = s_ref[inner, :] if is_own else ss[here, :]
            total = jnp.zeros((ROWS, NZ), jnp.float32)
            if is_own and step == 0:
                first = [v0_ref[inner, p * NZ : (p + 1) * NZ] for p in range(NP)]
                add_moments(0, inner, sum(v * v for v in first))
            for pair in range(NP // 2):
                wide = slice(pair * 2 * NZ, (pair + 1) * 2 * NZ)
                both = jnp.dot(weights, uh[step, around, wide], preferred_element_type=jnp.float32)
                low = jnp.dot(high_weights, ul[step, around, wide], preferred_element_type=jnp.float32)
                t = both[0 : 3 * ROWS] + (both[3 * ROWS :] + low)
                for q in range(2):
                    p = pair * 2 + q
                    lanes = slice(p * NZ, (p + 1) * NZ)
                    col = slice(q * NZ, (q + 1) * NZ)
                    g = (
                        pltpu.roll(t[0:ROWS, col], 1, 1)
                        + t[ROWS : 2 * ROWS, col]
                        + pltpu.roll(t[2 * ROWS :, col], NZ - 1, 1)
                    ) * scale
                    v0 = v0_ref[inner, lanes] if is_own else v0s[here, lanes]
                    if step == 0:
                        v = g
                        v1s[here, lanes] = v
                    elif step == 1:
                        v = 2.0 * g - v0
                    else:
                        v = 2.0 * g - v1s[here, lanes]
                        for y in range(NY):
                            result[plane - CX, pl.ds(p * NY + y, COMP, stride=NP * NY), :] = v[y * PAD : y * PAD + COMP]
                    if step < 2:
                        uh[step + 1, here, lanes], ul[step + 1, here, lanes] = split(scale * v)
                    if is_own:
                        total = total + v0 * v
            if step == 2:
                x = plane - CX
                writes.append(pltpu.make_async_copy(result.at[x].reshape(COMP * NP, NY, NZ), out_ref.at[:, x], sem.at[x]))
                writes[x].start()
            if is_own:
                add_moments(step + 1, inner, total)

    lane = lax.broadcasted_iota(jnp.int32, (4, NZ), 1)
    moments = jnp.zeros((4, NZ), jnp.float32)
    for j in range(WIN):
        stacked = jnp.concatenate([jnp.sum(sums[n][j], axis=0, keepdims=True) for n in range(4)], axis=0)
        value = jnp.sum(stacked, axis=1, keepdims=True)
        moments = moments + jnp.where(lane == ((window_of(idx) + j) & 127), value, 0.0)
    pm_ref[...] = jnp.broadcast_to(moments[None], pm_ref.shape)
    for write in writes:
        write.wait()


HBM = pl.BlockSpec(memory_space=pltpu.HBM)
VMEM = pl.BlockSpec(memory_space=pltpu.VMEM)
SMEM = pl.BlockSpec(memory_space=pltpu.SMEM)


def body(site_class, probe_signs, masses, force_blocks):
    payload = pl.pallas_call(
        payload_kernel,
        out_shape=pltpu.VMEM((PAY_ROWS, NZ), jnp.int32),
        in_specs=[HBM, HBM],
        out_specs=VMEM,
        scratch_shapes=[pltpu.SemaphoreType.DMA((2,))],
        cost_estimate=pl.CostEstimate(flops=0, bytes_accessed=800000, transcendentals=0),
        name="payload",
    )(probe_signs.reshape(COMP * NP * CX, NY, NZ), site_class.reshape(ATOMS * CX, NY, NZ))

    count = 64
    far = lax.ppermute(payload, SPACE, [(i, (i + 1) % count if i % 2 else (i - 1) % count) for i in range(count)])
    near = lax.ppermute(payload, SPACE, [(i, i ^ 1) for i in range(count)])

    prepared = pl.pallas_call(
        prepare_kernel,
        out_shape=(
            pltpu.VMEM((6 * ROWS, 3 * ROWS), jnp.bfloat16),
            pltpu.VMEM((8, NZ), jnp.float32),
            pltpu.VMEM((CX * ROWS, WIDE), jnp.bfloat16),
            pltpu.VMEM((CX * ROWS, WIDE), jnp.bfloat16),
            pltpu.VMEM((CX * ROWS, WIDE), jnp.float32),
            pltpu.VMEM((CX * ROWS, NZ), jnp.float32),
            pltpu.VMEM((CX * ROWS, NZ), jnp.int32),
        ),
        in_specs=[SMEM, VMEM, VMEM],
        out_specs=(VMEM,) * 7,
        scratch_shapes=[pltpu.VMEM((3 * ROWS, 3 * ROWS), jnp.float32)],
        cost_estimate=pl.CostEstimate(flops=1000000, bytes_accessed=300000, transcendentals=0),
        name="prepare",
    )(masses, force_blocks, payload)

    group = 32
    last, parts = pl.pallas_call(
        main_kernel,
        out_shape=(
            jax.ShapeDtypeStruct((COMP * NP, CX, NY, NZ), jnp.float32),
            jax.ShapeDtypeStruct((group, 4, NZ), jnp.float32),
        ),
        in_specs=[VMEM] * 9,
        out_specs=(pl.BlockSpec(memory_space=pltpu.HBM), VMEM),
        scratch_shapes=[
            pltpu.VMEM((3, PLANES * ROWS, WIDE), jnp.bfloat16),
            pltpu.VMEM((3, PLANES * ROWS, WIDE), jnp.bfloat16),
            pltpu.VMEM((PLANES * ROWS, WIDE), jnp.float32),
            pltpu.VMEM((PLANES * ROWS, WIDE), jnp.float32),
            pltpu.VMEM((PLANES * ROWS, NZ), jnp.float32),
            pltpu.VMEM((CX, SIGN_ROWS // CX, NZ), jnp.float32),
            pltpu.SemaphoreType.DMA((CX,)),
        ],
        compiler_params=pltpu.CompilerParams(vmem_limit_bytes=24 * 2**20),
        cost_estimate=pl.CostEstimate(flops=2000000000, bytes_accessed=2000000, transcendentals=0),
        name="chebyshev",
    )(near, far, *prepared)

    parts = lax.all_to_all(parts, NEAR, 0, 0, tiled=True).sum(0)
    parts = jnp.broadcast_to(parts[None], (lax.axis_size("z"), 4, NZ))
    moments = lax.all_to_all(parts, "z", 0, 0, tiled=True).sum(0) * (1.0 / 368640)
    return moments, last.reshape(COMP, NP, CX, NY, NZ)


def solution(mesh):
    fine = Mesh(mesh.devices.reshape(2, 16, 2, 2, 4), SPACE + PROBE)
    return jax.shard_map(
        body,
        mesh=fine,
        in_specs=(P(None, SPACE, None, None), P(None, PROBE, SPACE, None, None), P(), P()),
        out_specs=(P(), P(None, PROBE, SPACE, None, None)),
        check_vma=False,
    )
```

time: 63.1 us -> 58.3 us (0.924)
  blocking collectives: 15.9 us -> 35.3 us
  waiting for transfers between devices: 10.4 us -> 0.01 us
  starting transfers between devices: 23.5 us -> 15.2 us
  local copies, waits for them, and re-layouts: 5.99 us -> 0.01 us
    all_to_all x0 -> x1, blocking collectives: none -> 19.6 us  [body(): lax.all_to_all(parts, 'z', 0, 0, tiled=True).sum(0) * (1.0 / 368640)]
    all_to_all x1 -> x0, waiting for transfers between devices: 10.4 us -> none  [body(): lax.all_to_all(parts, 'z', 0, 0, tiled=True).sum(0) * (1.0 / 368640)]
    all_to_all x1 -> x0, starting transfers between devices: 8.29 us -> none  [body(): lax.all_to_all(parts, 'z', 0, 0, tiled=True).sum(0) * (1.0 / 368640)]
    unnamed x9 -> x2, local copies, waits for them, and re-layouts: 5.19 us -> 0.01 us
    pallas_call x2 -> x3, Pallas kernels: 5.51 us -> 6.1 us  [the longest x1 3.62 us: body(): pl.pallas_call(main_kernel, out_shape=(jax.ShapeDtypeStruct((COMP * NP, C...]
  transfers between devices with their start and end apart: 3 -> 2, of which waited for: 1 -> 0; matrix products, arithmetic and copies ran while one was open for 2% -> 0% of each run, Pallas kernels for 3% -> 3%
where the time goes in v2:
time: 58.3 us; the launch traced here: 58 us
  blocking collectives  35.3 us (61%)
  starting transfers between devices  15.2 us (26%)
  Pallas kernels  6.1 us (10%)
  between operations  0.7 us (1%)
  other arithmetic  0.65 us (1%)
    all_to_all x1, blocking collectives, body(): lax.all_to_all(parts, 'z', 0, 0, tiled=True).sum(0) * (1.0 / 368640)  19.6 us
    all_to_all x1, blocking collectives, body(): parts = lax.all_to_all(parts, NEAR, 0, 0, tiled=True).sum(0)  15.8 us
    ppermute x1, starting transfers between devices, body(): near = lax.ppermute(payload, SPACE, [(i, i ^ 1) for i in range(count)])  10.2 us
    ppermute x1, starting transfers between devices, body(): lax.ppermute(payload, SPACE, [(i, (i + 1) % count if i % 2 else (i - 1) %...  4.94 us
    pallas_call x1, Pallas kernels, body(): pl.pallas_call(main_kernel, out_shape=(jax.ShapeDtypeStruct((COMP * NP, C...  3.62 us
    pallas_call x1, Pallas kernels, body(): pl.pallas_call(prepare_kernel, out_shape=(pltpu.VMEM((6 * ROWS, 3 * ROWS)...  1.47 us
  transfers between devices with their start and end apart: 2, of which 0 were waited for; matrix products, arithmetic and copies ran while one was open for 0% of the time, Pallas kernels for 3%

profile of v2, /device:TPU:1, one launch (start us, length us, event | category | flops | bytes accessed | tf_op | source)
XLA Modules:
  0.0 58.0 jit_solution(3330395353899460964)
XLA Ops:
  0.6 1.0 %payload.1.own_ref = s32[780,128]{1,0:T(8,128)S(1)} custom-call(s32[360,2,128]{2,1,0:T(2,128)} %bitcast.3, s32[30,2,128]{2,1,0:T(2,128)} %bitcast.4), custom_call_target="tpu_custom_call" | custom-call | bytes 800000 | tf_op jit(solution)/shard_map/payload/pallas_call | solution.py:204
  1.6 0.0 copy-start
  1.7 4.9 %collective-permute-start.1 = (s32[780,128]{1,0:T(8,128)S(1)}, s32[780,128]{1,0:T(8,128)S(1)}, u32[]{:S(2)}, u32[]{:S(2)}) collective-permute-start(s32[780,128]{1,0:T(8,128)S(1)} %payload.1.own_ref), channel_id=1, source_target_pairs={{0,504},{8,16},{16,8},{24,32},{32,24},{40,48},{48,40},{56,64},{64,... | collective-permute-start | bytes 1198088 | tf_op jit(solution)/shard_map/ppermute | solution.py:215
  6.6 10.2 %collective-permute-start = (s32[780,128]{1,0:T(8,128)S(1)}, s32[780,128]{1,0:T(8,128)S(1)}, u32[]{:S(2)}, u32[]{:S(2)}) collective-permute-start(s32[780,128]{1,0:T(8,128)S(1)} %payload.1.own_ref), channel_id=1, source_target_pairs={{0,8},{8,0},{16,24},{24,16},{32,40},{40,32},{48,56},{56,48},{64,72... | collective-permute-start | bytes 1198088 | tf_op jit(solution)/shard_map/ppermute | solution.py:216
  16.9 0.0 copy-done
  16.9 1.5 %prepare.1 = (bf16[384,192]{1,0:T(8,128)(2,1)S(1)}, f32[8,128]{1,0:T(8,128)S(1)}, bf16[192,512]{1,0:T(8,128)(2,1)S(1)}, bf16[192,512]{1,0:T(8,128)(2,1)S(1)}, f3...) custom-call(f32[128]{0:T(128)} %mass_ref.1, f32[27,30,30]{2,1,0:T(8,128)} %fb_ref.1, ...), custom_call_target="tpu_custom_call" | custom-call | flops 1000000 | bytes 300000 | tf_op jit(solution)/shard_map/prepare/pallas_call | solution.py:218
  18.3 0.0 collective-permute-done.1.b_ref
  18.4 0.0 collective-permute-done.a_ref
  18.4 3.6 %chebyshev.1 = (f32[120,3,2,128]{3,2,1,0:T(2,128)}, f32[32,4,128]{2,1,0:T(4,128)S(1)}) custom-call(s32[780,128]{1,0:T(8,128)S(1)} %collective-permute-done.a_ref, s32[780,128]{1,0:T(8,128)S(1)} %collective-permute-done.1.b_ref, bf16[384,192]{1,0:T(8,128)(2,1)S(1)} %get-tuple-element.11.w_ref, f32[8,128]{1,0:T(8,128)S(1)} %get-tuple-element.12.inv_ref, ...), custom_call_target="tpu_custom_call" | custom-call | flops 2000000000 | bytes 2000000 | tf_op jit(solution)/shard_map/chebyshev/pallas_call | solution.py:237
  22.0 15.8 %all_to_all.10 = f32[32,4,128]{2,1,0:T(4,128)S(1)} all-to-all(f32[32,4,128]{2,1,0:T(4,128)S(1)} %get-tuple-element.18), channel_id=1, replica_groups=mesh['xl'=2,'z'=16,'core'=2,'xh'=2,'y'=4] {'xl','core','xh','y'}, dimensions={0} | all-to-all | bytes 131072 | tf_op jit(solution)/shard_map/all_to_all | solution.py:259
  37.8 19.6 %all_to_all.11 = f32[16,4,128]{2,1,0:T(4,128)S(1)} all-to-all(f32[16,4,128]{2,1,0:T(4,128)S(1)} %broadcast_in_dim.2), channel_id=1, replica_groups=mesh['xl'=2,'z'=16,'core'=2,'xh'=2,'y'=4] {'z'}, dimensions={0} | all-to-all | bytes 65536 | tf_op jit(solution)/shard_map/all_to_all | solution.py:261
  57.4 0.6 %broadcast_multiply_fusion = f32[4,128]{1,0:T(4,128)} fusion(f32[4,128]{1,0:T(4,128)S(1)} %reduce_sum.19), kind=kLoop, calls=%fused_computation | loop fusion | flops 512 | bytes 4096 | tf_op jit(solution)/shard_map/mul | solution.py:261
  (3 shorter events, 0.1 us)
Async XLA Ops:
  1.6 15.2 %copy-start = (s32[780,128]{1,0:T(8,128)}, s32[780,128]{1,0:T(8,128)S(1)}, u32[]{:S(2)}) copy-start(s32[780,128]{1,0:T(8,128)S(1)} %payload.1.own_ref) | copy-start | bytes 1198084
  1.7 16.7 %collective-permute-start.1 = (s32[780,128]{1,0:T(8,128)S(1)}, s32[780,128]{1,0:T(8,128)S(1)}, u32[]{:S(2)}, u32[]{:S(2)}) collective-permute-start(s32[780,128]{1,0:T(8,128)S(1)} %payload.1.own_ref), channel_id=1, source_target_pairs={{0,504},{8,16},{16,8},{24,32},{32,24},{40,48},{48,40},{56,64},{64,... | collective-permute-start | bytes 1198088 | tf_op jit(solution)/shard_map/ppermute | solution.py:215
  6.6 11.8 %collective-permute-start = (s32[780,128]{1,0:T(8,128)S(1)}, s32[780,128]{1,0:T(8,128)S(1)}, u32[]{:S(2)}, u32[]{:S(2)}) collective-permute-start(s32[780,128]{1,0:T(8,128)S(1)} %payload.1.own_ref), channel_id=1, source_target_pairs={{0,8},{8,0},{16,24},{24,16},{32,40},{40,32},{48,56},{56,48},{64,72... | collective-permute-start | bytes 1198088 | tf_op jit(solution)/shard_map/ppermute | solution.py:216

commit v3 on v2

v3 whole, which is shorter than its diff:
```python
import jax
import jax.numpy as jnp
from jax import lax
from jax.experimental import pallas as pl
from jax.experimental.pallas import tpu as pltpu
from jax.sharding import Mesh, PartitionSpec as P

SPACE = ("xl", "z", "core")
PROBE = ("xh", "y")
NEAR = ("xl", "core", "xh", "y")

COMP, PAD = 30, 32
ATOMS, ATOM_PAD = 10, 16
NP, CX, NY, NZ = 4, 3, 2, 128
CELLS = CX * NY
ROWS = NY * PAD
WIDE = NP * NZ
SIGN_ROWS = COMP * NP * CELLS
LABEL_ROWS = ATOMS * CELLS
PAY_ROWS = SIGN_ROWS + LABEL_ROWS
PAY_PAD = PAY_ROWS + 4
WIN = 4
BAND = 3 * PAD
HALF = (2, 2)


def split(u):
    hi = u.astype(jnp.bfloat16)
    return hi, (u - hi.astype(jnp.float32)).astype(jnp.bfloat16)


def window_of(idx):
    return 2 * (idx & 63)


def own_index():
    return (lax.axis_index("xl") * lax.axis_size("z") + lax.axis_index("z")) * 2 + lax.axis_index("core")


def turned(k):
    return jnp.where(lax.axis_index("core") == 0, k, 2 - k)


def neighbour(slab):
    return own_index() + jnp.where(lax.axis_index("core") == 0, slab - 1, 1 - slab)


def store_scaled(u_ref, at, lanes, scales, fields):
    first, second = scales[0] * fields[0], scales[1] * fields[1]
    for sign, u in enumerate((first + second, first - second)):
        u_ref[sign, 0, at, lanes], u_ref[sign, 1, at, lanes] = split(u)


def load_slab(pay_ref, base, inv, u_ref, v0_ref, s_ref, rel_ref=None, offset=0):
    spread = (
        lax.broadcasted_iota(jnp.int32, (PAD, ATOM_PAD), 0) // 3
        == lax.broadcasted_iota(jnp.int32, (PAD, ATOM_PAD), 1)
    ).astype(jnp.bfloat16)
    valid = lax.broadcasted_iota(jnp.int32, (PAD, NZ), 0) < COMP
    cell = [turned(i // NY) * NY + i % NY for i in range(CELLS)]
    labels = jnp.concatenate(
        [pay_ref[pl.ds(offset + SIGN_ROWS + cell[i], ATOMS, stride=CELLS), :] for i in range(CELLS)], axis=1
    )
    labels = jnp.concatenate([labels, jnp.zeros((ATOM_PAD - ATOMS, CELLS * NZ), jnp.int32)], axis=0)
    labels = jnp.dot(spread, labels.astype(jnp.float32).astype(jnp.bfloat16), preferred_element_type=jnp.float32)
    rel = (labels.astype(jnp.int32) - base) & 127
    for x in range(CX):
        scales = []
        for y in range(NY):
            i = x * NY + y
            part = rel[:, i * NZ : (i + 1) * NZ]
            scale = jnp.where(part == 0, inv[0], jnp.where(part == 1, inv[1], jnp.where(part == 2, inv[2], inv[3])))
            scales.append(jnp.where(valid, scale, 0.0))
            at = slice(i * PAD, (i + 1) * PAD)
            s_ref[at, :] = scales[y]
            if rel_ref is not None:
                rel_ref[at, :] = jnp.where(valid, part, -1)
        for p in range(NP):
            lanes = slice(p * NZ, (p + 1) * NZ)
            fields = []
            for y in range(NY):
                i = x * NY + y
                sign = pay_ref[pl.ds(offset + p * CELLS + cell[i], COMP, stride=NP * CELLS), :]
                sign = jnp.concatenate([sign, jnp.zeros((PAD - COMP, NZ), jnp.int32)], axis=0)
                fields.append((2 * sign - 1).astype(jnp.float32))
                v0_ref[i * PAD : (i + 1) * PAD, lanes] = fields[y]
            store_scaled(u_ref, slice(x * PAD, (x + 1) * PAD), lanes, scales, fields)


def stencil(w_ref, planes, pair):
    lanes = slice(pair * 2 * NZ, (pair + 1) * 2 * NZ)
    sums = []
    for sign in range(2):
        field = jnp.concatenate(
            [ref[sign, part, at * PAD : (at + 1) * PAD, lanes] for part in range(2) for ref, at in planes], axis=0
        )
        t = jnp.dot(w_ref[sign], field, preferred_element_type=jnp.float32)
        o = t[0:BAND] + t[BAND:]
        sums.append(
            [
                pltpu.roll(o[0:PAD, c], 1, 1) + o[PAD : 2 * PAD, c] + pltpu.roll(o[2 * PAD :, c], NZ - 1, 1)
                for c in (slice(0, NZ), slice(NZ, 2 * NZ))
            ]
        )
    even, odd = sums
    return [(even[q] + odd[q], even[q] - odd[q]) for q in range(2)]


def cell_rows(ref, plane, lanes):
    return [ref[(plane * NY + y) * PAD : (plane * NY + y + 1) * PAD, lanes] for y in range(NY)]


ALL = slice(None)


class Moments:
    def __init__(self, rel_ref, v0_ref):
        self.rel_ref, self.v0_ref, self.sums = rel_ref, v0_ref, {}

    def add(self, n, x, fields):
        rels = cell_rows(self.rel_ref, x, ALL)
        for y in range(NY):
            total = 0.0
            for p, field in enumerate(fields):
                total = total + cell_rows(self.v0_ref, x, slice(p * NZ, (p + 1) * NZ))[y] * field[y]
            for j in range(WIN):
                picked = jnp.where(rels[y] == j, total, 0.0)
                part = sum(picked[8 * k : 8 * k + 8] for k in range(PAD // 8))
                self.sums[n, j] = self.sums[n, j] + part if (n, j) in self.sums else part


def payload_kernel(signs_ref, labels_ref, pay_ref, sems):
    copies = [
        pltpu.make_async_copy(signs_ref.reshape(SIGN_ROWS, NZ), pay_ref.at[0:SIGN_ROWS, :], sems.at[0]),
        pltpu.make_async_copy(labels_ref.reshape(LABEL_ROWS, NZ), pay_ref.at[SIGN_ROWS:PAY_ROWS, :], sems.at[1]),
    ]
    for copy in copies:
        copy.start()
    for copy in copies:
        copy.wait()


def prepare_kernel(mass_ref, fb_ref, own_ref, w_ref, inv_ref, u_ref, v0_ref, s_ref, rel_ref, again_ref, full):
    for k in range(2):
        again_ref[k * PAY_PAD : (k + 1) * PAY_PAD, :] = own_ref[...]
    full[...] = jnp.zeros_like(full)
    for k in range(3):
        dx = turned(k)
        for dz in range(3):
            same = fb_ref[9 * dx + 3 + dz]
            other = fb_ref[9 * dx + dz] + fb_ref[9 * dx + 6 + dz]
            r, c = dz * PAD, k * PAD
            full[0, r : r + COMP, c : c + COMP] = 0.5 * (same + other)
            full[1, r : r + COMP, c : c + COMP] = 0.5 * (same - other)
    for sign in range(2):
        hi, lo = split(full[sign])
        w_ref[sign, 0:BAND, :] = jnp.concatenate([hi[:, 0:BAND], hi[:, 0:BAND]], axis=1)
        w_ref[sign, BAND:, :] = jnp.concatenate([lo[:, 0:BAND], jnp.zeros((BAND, BAND), jnp.bfloat16)], axis=1)

    for slab in range(3):
        base = window_of(neighbour(slab))
        inv = [1.0 / jnp.sqrt(jnp.full((1, NZ), mass_ref[(base + j) & 127], jnp.float32)) for j in range(WIN)]
        if slab == 1:
            load_slab(own_ref, base, inv, u_ref, v0_ref, s_ref, rel_ref)
        else:
            for j in range(WIN):
                at = slab * 2 + j
                inv_ref[at : at + 1, :] = inv[j]


def near_kernel(pay_ref, w_ref, inv_ref, u0, v0, s, rel, u1_ref, u2_ref, v1_ref, sums_ref, u0n, v0n, sn):
    inv = [inv_ref[4 + j : 5 + j, :] for j in range(WIN)]
    offset = (1 - lax.axis_index("core")) * PAY_PAD
    load_slab(pay_ref, window_of(neighbour(2)), inv, u0n, v0n, sn, offset=offset)
    moments = Moments(rel, v0)
    lanes_of = [slice(p * NZ, (p + 1) * NZ) for p in range(NP)]
    for x in range(CX):
        moments.add(0, x, [cell_rows(v0, x, lanes_of[p]) for p in range(NP)])

    def first(plane):
        return (u0, plane - 3) if plane < 6 else (u0n, plane - 6)

    def scales_of(plane):
        return cell_rows(s, plane - 3, ALL) if plane < 6 else cell_rows(sn, plane - 6, ALL)

    for plane in (4, 5, 6, 7):
        scales, fields = scales_of(plane), []
        for pair in range(NP // 2):
            for q, g in enumerate(stencil(w_ref, [first(plane + d) for d in (-1, 0, 1)], pair)):
                lanes = lanes_of[2 * pair + q]
                v = [scales[y] * g[y] for y in range(NY)]
                store_scaled(u1_ref, slice((plane - 4) * PAD, (plane - 3) * PAD), lanes, scales, v)
                fields.append(v)
                if plane < 6:
                    for y in range(NY):
                        at = (plane - 4) * ROWS + y * PAD
                        v1_ref[at : at + PAD, lanes] = v[y]
        if plane < 6:
            moments.add(1, plane - 3, fields)
    for plane in (5, 6):
        scales, fields = scales_of(plane), []
        for pair in range(NP // 2):
            for q, g in enumerate(stencil(w_ref, [(u1_ref, plane - 4 + d) for d in (-1, 0, 1)], pair)):
                lanes = lanes_of[2 * pair + q]
                before = cell_rows(v0, 2, lanes) if plane == 5 else cell_rows(v0n, 0, lanes)
                v = [2.0 * (scales[y] * g[y]) - before[y] for y in range(NY)]
                store_scaled(u2_ref, slice((plane - 5) * PAD, (plane - 4) * PAD), lanes, scales, v)
                fields.append(v)
        if plane == 5:
            moments.add(2, 2, fields)
    for n in range(4):
        for j in range(WIN):
            at = (n * WIN + j) * 8
            sums_ref[at : at + 8, :] = moments.sums.get((n, j), jnp.zeros((8, NZ), jnp.float32))


def far_kernel(
    pay_ref, w_ref, inv_ref, u0, v0, s, rel, u1, u2, v1, sums_ref, out_ref, pm_ref, u0f, v0f, sf, u1f, u2f, v1f
):
    inv = [inv_ref[j : j + 1, :] for j in range(WIN)]
    load_slab(pay_ref, window_of(neighbour(0)), inv, u0f, v0f, sf)
    moments = Moments(rel, v0)
    for n in range(4):
        for j in range(WIN):
            at = (n * WIN + j) * 8
            moments.sums[n, j] = sums_ref[at : at + 8, :]
    lanes_of = [slice(p * NZ, (p + 1) * NZ) for p in range(NP)]

    def source(step, plane):
        if step == 0:
            return (u0f, plane) if plane < 3 else (u0, plane - 3)
        if step == 1:
            return (u1f, plane - 1) if plane < 4 else (u1, plane - 4)
        return (u2f, plane - 2) if plane < 5 else (u2, plane - 5)

    flat = out_ref.reshape(SIGN_ROWS, NZ)
    for step in range(3):
        for plane in range(step + 1, step + 4):
            own = plane >= 3
            scales = cell_rows(s, plane - 3, ALL) if own else cell_rows(sf, plane, ALL)
            fields = []
            for pair in range(NP // 2):
                planes = [source(step, plane + d) for d in (-1, 0, 1)]
                for q, g in enumerate(stencil(w_ref, planes, pair)):
                    p = 2 * pair + q
                    lanes = lanes_of[p]
                    v = [scales[y] * g[y] for y in range(NY)]
                    if step == 1:
                        before = cell_rows(v0, plane - 3, lanes) if own else cell_rows(v0f, plane, lanes)
                        v = [2.0 * v[y] - before[y] for y in range(NY)]
                    elif step == 2:
                        before = cell_rows(v1f, 0, lanes) if plane == 3 else cell_rows(v1, plane - 4, lanes)
                        v = [2.0 * v[y] - before[y] for y in range(NY)]
                    if step == 0 and own:
                        for y in range(NY):
                            v1f[y * PAD : (y + 1) * PAD, lanes] = v[y]
                    if step < 2:
                        at = plane - 1 - step
                        store_scaled((u1f, u2f)[step], slice(at * PAD, (at + 1) * PAD), lanes, scales, v)
                    else:
                        for y in range(NY):
                            start = p * CELLS + turned(plane - 3) * NY + y
                            flat[pl.ds(start, COMP, stride=NP * CELLS), :] = v[y][0:COMP]
                    fields.append(v)
            if own:
                moments.add(step + 1, plane - 3, fields)

    lane = lax.broadcasted_iota(jnp.int32, (4, NZ), 1)
    total = jnp.zeros((4, NZ), jnp.float32)
    for j in range(WIN):
        stacked = jnp.concatenate([jnp.sum(moments.sums[n, j], axis=0, keepdims=True) for n in range(4)], axis=0)
        value = jnp.sum(stacked, axis=1, keepdims=True)
        total = total + jnp.where(lane == ((window_of(own_index()) + j) & 127), value, 0.0)
    pm_ref[...] = jnp.broadcast_to(total[None], pm_ref.shape)


HBM = pl.BlockSpec(memory_space=pltpu.HBM)
VMEM = pl.BlockSpec(memory_space=pltpu.VMEM)
SMEM = pl.BlockSpec(memory_space=pltpu.SMEM)


def body(site_class, probe_signs, masses, force_blocks):
    payload = pl.pallas_call(
        payload_kernel,
        out_shape=pltpu.VMEM((PAY_PAD, NZ), jnp.int32),
        in_specs=[HBM, HBM],
        out_specs=VMEM,
        scratch_shapes=[pltpu.SemaphoreType.DMA((2,))],
        cost_estimate=pl.CostEstimate(flops=0, bytes_accessed=800000, transcendentals=0),
        name="payload",
    )(probe_signs.reshape(COMP * NP * CX, NY, NZ), site_class.reshape(ATOMS * CX, NY, NZ))

    count = 64
    far = lax.ppermute(payload, SPACE, [(i, (i + 1) % count if i % 2 else (i - 1) % count) for i in range(count)])
    slab = HALF + (BAND, WIDE)
    *prepared, again = pl.pallas_call(
        prepare_kernel,
        out_shape=(
            pltpu.VMEM((2, 2 * BAND, 2 * BAND), jnp.bfloat16),
            pltpu.VMEM((8, NZ), jnp.float32),
            pltpu.VMEM(slab, jnp.bfloat16),
            pltpu.VMEM((CX * ROWS, WIDE), jnp.float32),
            pltpu.VMEM((CX * ROWS, NZ), jnp.float32),
            pltpu.VMEM((CX * ROWS, NZ), jnp.int32),
            pltpu.VMEM((2 * PAY_PAD, NZ), jnp.int32),
        ),
        in_specs=[SMEM, VMEM, VMEM],
        out_specs=(VMEM,) * 7,
        scratch_shapes=[pltpu.VMEM((2, BAND, NZ), jnp.float32)],
        cost_estimate=pl.CostEstimate(flops=1000000, bytes_accessed=300000, transcendentals=0),
        name="prepare",
    )(masses, force_blocks, payload)
    near = lax.all_to_all(again, "core", 0, 0, tiled=True)

    shared = pl.pallas_call(
        near_kernel,
        out_shape=(
            pltpu.VMEM(HALF + (4 * PAD, WIDE), jnp.bfloat16),
            pltpu.VMEM(HALF + (2 * PAD, WIDE), jnp.bfloat16),
            pltpu.VMEM((2 * ROWS, WIDE), jnp.float32),
            pltpu.VMEM((16 * 8, NZ), jnp.float32),
        ),
        in_specs=[VMEM] * 7,
        out_specs=(VMEM,) * 4,
        scratch_shapes=[
            pltpu.VMEM(slab, jnp.bfloat16),
            pltpu.VMEM((CX * ROWS, WIDE), jnp.float32),
            pltpu.VMEM((CX * ROWS, NZ), jnp.float32),
        ],
        compiler_params=pltpu.CompilerParams(vmem_limit_bytes=24 * 2**20),
        cost_estimate=pl.CostEstimate(flops=800000000, bytes_accessed=1000000, transcendentals=0),
        name="near_part",
    )(near, *prepared)

    group = 32
    last, parts = pl.pallas_call(
        far_kernel,
        out_shape=(
            pltpu.VMEM((COMP * NP, CX, NY, NZ), jnp.float32),
            pltpu.VMEM((group, 4, NZ), jnp.float32),
        ),
        in_specs=[VMEM] * 11,
        out_specs=(VMEM, VMEM),
        scratch_shapes=[
            pltpu.VMEM(slab, jnp.bfloat16),
            pltpu.VMEM((CX * ROWS, WIDE), jnp.float32),
            pltpu.VMEM((CX * ROWS, NZ), jnp.float32),
            pltpu.VMEM(slab, jnp.bfloat16),
            pltpu.VMEM(slab, jnp.bfloat16),
            pltpu.VMEM((ROWS, WIDE), jnp.float32),
        ],
        compiler_params=pltpu.CompilerParams(vmem_limit_bytes=24 * 2**20),
        cost_estimate=pl.CostEstimate(flops=1200000000, bytes_accessed=2000000, transcendentals=0),
        name="far_part",
    )(far, *prepared, *shared)

    parts = lax.all_to_all(parts, NEAR, 0, 0, tiled=True).sum(0)
    parts = jnp.broadcast_to(parts[None], (lax.axis_size("z"), 4, NZ))
    moments = lax.all_to_all(parts, "z", 0, 0, tiled=True).sum(0) * (1.0 / 368640)
    return moments, last.reshape(COMP, NP, CX, NY, NZ)


def solution(mesh):
    fine = Mesh(mesh.devices.reshape(2, 16, 2, 2, 4), SPACE + PROBE)
    return jax.shard_map(
        body,
        mesh=fine,
        in_specs=(P(None, SPACE, None, None), P(None, PROBE, SPACE, None, None), P(), P()),
        out_specs=(P(), P(None, PROBE, SPACE, None, None)),
        check_vma=False,
    )
```

time: 58.3 us -> 57.5 us (0.986)
  waiting for transfers between devices: 0.01 us -> 10.7 us
  blocking collectives: 35.3 us -> 26.4 us
  starting transfers between devices: 15.2 us -> 11.7 us
  local copies, waits for them, and re-layouts: 0.01 us -> 1.36 us
    all_to_all x0 -> x1, waiting for transfers between devices: none -> 10.7 us  [body(): lax.all_to_all(parts, 'z', 0, 0, tiled=True).sum(0) * (1.0 / 368640)]
    ppermute x1 -> x0, starting transfers between devices: 10.2 us -> none  [body(): near = lax.ppermute(payload, SPACE, [(i, i ^ 1) for i in range(count)])]
    all_to_all x1, blocking collectives: 19.6 us -> 12.3 us  [body(): near = lax.all_to_all(again, 'core', 0, 0, tiled=True)]
    all_to_all x0 -> x1, starting transfers between devices: none -> 6.77 us  [body(): lax.all_to_all(parts, 'z', 0, 0, tiled=True).sum(0) * (1.0 / 368640)]
    all_to_all x1, blocking collectives: 15.8 us -> 14 us  [body(): parts = lax.all_to_all(parts, NEAR, 0, 0, tiled=True).sum(0)]
    unnamed x2 -> x3, local copies, waits for them, and re-layouts: 0.01 us -> 0.74 us
    broadcast_in_dim x1, local copies, waits for them, and re-layouts: 0.01 us -> 0.61 us  [body(): parts = jnp.broadcast_to(parts[None], (lax.axis_size('z'), 4, NZ))]
    pallas_call x3 -> x4, Pallas kernels: 6.1 us -> 5.66 us  [the longest x1 1.99 us: body(): pl.pallas_call(far_kernel, out_shape=(pltpu.VMEM((COMP * NP, CX, NY, NZ),...]
  transfers between devices with their start and end apart: 2 -> 2, of which waited for: 0 -> 1; matrix products, arithmetic and copies ran while one was open for 0% -> 1% of each run, Pallas kernels for 3% -> 5%
where the time goes in v3:
time: 57.5 us; the launch traced here: 57.2 us
  blocking collectives  26.4 us (46%)
  starting transfers between devices  11.7 us (20%)
  waiting for transfers between devices  10.7 us (19%)
  Pallas kernels  5.66 us (10%)
  local copies, waits for them, and re-layouts  1.36 us (2%)
  between operations  0.7 us (1%)
  other arithmetic  0.65 us (1%)
    all_to_all x1, blocking collectives, body(): parts = lax.all_to_all(parts, NEAR, 0, 0, tiled=True).sum(0)  14 us
    all_to_all x1, blocking collectives, body(): near = lax.all_to_all(again, 'core', 0, 0, tiled=True)  12.3 us
    all_to_all x1, waiting for transfers between devices, body(): lax.all_to_all(parts, 'z', 0, 0, tiled=True).sum(0) * (1.0 / 368640)  10.7 us
    all_to_all x1, starting transfers between devices, body(): lax.all_to_all(parts, 'z', 0, 0, tiled=True).sum(0) * (1.0 / 368640)  6.77 us
    ppermute x1, starting transfers between devices, body(): lax.ppermute(payload, SPACE, [(i, (i + 1) % count if i % 2 else (i - 1) %...  4.94 us
    pallas_call x1, Pallas kernels, body(): pl.pallas_call(far_kernel, out_shape=(pltpu.VMEM((COMP * NP, CX, NY, NZ),...  1.99 us
    pallas_call x1, Pallas kernels, body(): pl.pallas_call(prepare_kernel, out_shape=(pltpu.VMEM((2, 2 * BAND, 2 * BA...  1.48 us
    pallas_call x1, Pallas kernels, body(): pl.pallas_call(near_kernel, out_shape=(pltpu.VMEM(HALF + (4 * PAD, WIDE),...  1.17 us
  transfers between devices with their start and end apart: 2, of which 1 were waited for; matrix products, arithmetic and copies ran while one was open for 1% of the time, Pallas kernels for 5%

profile of v3, /device:TPU:1, one launch (start us, length us, event | category | flops | bytes accessed | tf_op | source)
XLA Modules:
  0.0 57.2 jit_solution(10043291099485723740)
XLA Ops:
  0.6 1.0 %payload.1.own_ref = s32[784,128]{1,0:T(8,128)S(1)} custom-call(s32[360,2,128]{2,1,0:T(2,128)} %bitcast.8, s32[30,2,128]{2,1,0:T(2,128)} %bitcast.9), custom_call_target="tpu_custom_call" | custom-call | bytes 800000 | tf_op jit(solution)/shard_map/payload/pallas_call | solution.py:283
  1.6 0.0 copy-start
  1.7 4.9 %collective-permute-start = (s32[784,128]{1,0:T(8,128)S(1)}, s32[784,128]{1,0:T(8,128)S(1)}, u32[]{:S(2)}, u32[]{:S(2)}) collective-permute-start(s32[784,128]{1,0:T(8,128)S(1)} %payload.1.own_ref), channel_id=1, source_target_pairs={{0,504},{8,16},{16,8},{24,32},{32,24},{40,48},{48,40},{56,64},{64,... | collective-permute-start | bytes 1204232 | tf_op jit(solution)/shard_map/ppermute | solution.py:294
  6.6 0.0 copy-done
  6.6 1.5 %prepare.1 = (bf16[2,192,192]{2,1,0:T(8,128)(2,1)S(1)}, f32[8,128]{1,0:T(8,128)S(1)}, bf16[2,2,96,512]{3,2,1,0:T(8,128)(2,1)S(1)}, f32[192,512]{1,0:T(8,128)S(1)...) custom-call(f32[128]{0:T(128)} %mass_ref.1, f32[27,30,30]{2,1,0:T(8,128)} %fb_ref.1, ...), custom_call_target="tpu_custom_call" | custom-call | flops 1000000 | bytes 300000 | tf_op jit(solution)/shard_map/prepare/pallas_call | solution.py:296
  8.1 12.3 %all_to_all.21 = s32[2,784,128]{2,1,0:T(8,128)S(1)} all-to-all(s32[2,784,128]{2,1,0:T(8,128)S(1)} %bitcast.6), channel_id=1, replica_groups=mesh['xl'=2,'z'=16,'core'=2,'xh'=2,'y'=4] {'core'}, dimensions={0} | all-to-all | bytes 1605632 | tf_op jit(solution)/shard_map/all_to_all | solution.py:313
  20.4 1.2 %near_part.1 = (bf16[2,2,128,512]{3,2,1,0:T(8,128)(2,1)S(1)}, bf16[2,2,64,512]{3,2,1,0:T(8,128)(2,1)S(1)}, f32[128,512]{1,0:T(8,128)S(1)}, f32[128,128]{1,0:T(8,128)S(1)}) custom-call(s32[1568,128]{1,0:T(8,128)S(1)} %bitcast.7, bf16[2,192,192]{2,1,0:T(8,128)(2,1)S(1)} %get-tuple-element.15.w_ref, f32[8,128]{1,0:T(8,128)S(1)} %get-tuple-element.16.inv_ref, ...), custom_call_target="tpu_custom_call" | custom-call | flops 800000000 | bytes 1000000 | tf_op jit(solution)/shard_map/near_part/pallas_call | solution.py:315
  21.6 0.0 collective-permute-done.pay_ref
  21.6 2.0 %far_part.1 = (f32[120,3,2,128]{3,2,1,0:T(2,128)S(1)}, f32[32,4,128]{2,1,0:T(4,128)S(1)}) custom-call(s32[784,128]{1,0:T(8,128)S(1)} %collective-permute-done.pay_ref, bf16[2,192,192]{2,1,0:T(8,128)(2,1)S(1)} %get-tuple-element.15.w_ref, f32[8,128]{1,0:T(8,128)S(1)} %get-tuple-element.16.inv_ref, bf16[2,2,96,512]{3,2,1,0:T(8,128)(2,1)S(1)} %get-tuple-element.17.u0, ...), custom_call_target="tpu_custom_call" | custom-call | flops 1200000000 | bytes 2000000 | tf_op jit(solution)/shard_map/far_part/pallas_call | solution.py:336
  23.6 14.0 %all_to_all.22 = f32[32,4,128]{2,1,0:T(4,128)S(1)} all-to-all(f32[32,4,128]{2,1,0:T(4,128)S(1)} %get-tuple-element.26), channel_id=1, replica_groups=mesh['xl'=2,'z'=16,'core'=2,'xh'=2,'y'=4] {'xl','core','xh','y'}, dimensions={0} | all-to-all | bytes 131072 | tf_op jit(solution)/shard_map/all_to_all | solution.py:357
  37.7 0.6 %broadcast_in_dim.2 = f32[16,4,128]{2,1,0:T(4,128)} broadcast(f32[4,128]{1,0:T(4,128)S(1)} %reduce_sum.18), dimensions={1,2} | broadcast | bytes 34816 | tf_op jit(solution)/shard_map/broadcast_in_dim | solution.py:358
  38.3 6.8 %all-to-all-start.2 = ((f32[16,4,128]{2,1,0:T(4,128)}), f32[16,4,128]{2,1,0:T(4,128)S(1)}, u32[]{:S(2)}, u32[]{:S(2)}) async-start(f32[16,4,128]{2,1,0:T(4,128)} %broadcast_in_dim.2), calls=%async_computation.2 | async-start | bytes 65536 | tf_op jit(solution)/shard_map/all_to_all | solution.py:359
  45.1 0.7 %copy.8 = f32[30,4,3,2,128]{4,3,2,1,0:T(2,128)} copy(f32[30,4,3,2,128]{4,3,2,1,0:T(2,128)S(1)} %bitcast.5) | data formatting | bytes 737280
  45.8 10.7 %all-to-all-done.2 = f32[16,4,128]{2,1,0:T(4,128)S(1)} async-done(((f32[16,4,128]{2,1,0:T(4,128)}), f32[16,4,128]{2,1,0:T(4,128)S(1)}, u32[]{:S(2)}, u32[]{:S(2)}) %all-to-all-start.2) | async-done | bytes 32800 | tf_op jit(solution)/shard_map/all_to_all | solution.py:359
  56.6 0.6 %broadcast_multiply_fusion = f32[4,128]{1,0:T(4,128)} fusion(f32[4,128]{1,0:T(4,128)S(1)} %reduce_sum.19), kind=kLoop, calls=%fused_computation | loop fusion | flops 512 | bytes 4096 | tf_op jit(solution)/shard_map/mul | solution.py:359
  (2 shorter events, 0.1 us)
Async XLA Ops:
  1.6 5.0 %copy-start = (s32[784,128]{1,0:T(8,128)}, s32[784,128]{1,0:T(8,128)S(1)}, u32[]{:S(2)}) copy-start(s32[784,128]{1,0:T(8,128)S(1)} %payload.1.own_ref) | copy-start | bytes 1204228
  1.7 19.9 %collective-permute-start = (s32[784,128]{1,0:T(8,128)S(1)}, s32[784,128]{1,0:T(8,128)S(1)}, u32[]{:S(2)}, u32[]{:S(2)}) collective-permute-start(s32[784,128]{1,0:T(8,128)S(1)} %payload.1.own_ref), channel_id=1, source_target_pairs={{0,504},{8,16},{16,8},{24,32},{32,24},{40,48},{48,40},{56,64},{64,... | collective-permute-start | bytes 1204232 | tf_op jit(solution)/shard_map/ppermute | solution.py:294
  38.3 18.3 %all-to-all-start.2 = ((f32[16,4,128]{2,1,0:T(4,128)}), f32[16,4,128]{2,1,0:T(4,128)S(1)}, u32[]{:S(2)}, u32[]{:S(2)}) async-start(f32[16,4,128]{2,1,0:T(4,128)} %broadcast_in_dim.2), calls=%async_computation.2 | async-start | bytes 65536 | tf_op jit(solution)/shard_map/all_to_all | solution.py:359

commit v4 on v3

--- a/solution.py
+++ b/solution.py
@@ -121,7 +121,7 @@
         rels = cell_rows(self.rel_ref, x, ALL)
         for y in range(NY):
             total = 0.0
-            for p, field in enumerate(fields):
+            for p, field in fields.items():
                 total = total + cell_rows(self.v0_ref, x, slice(p * NZ, (p + 1) * NZ))[y] * field[y]
             for j in range(WIN):
                 picked = jnp.where(rels[y] == j, total, 0.0)
@@ -175,7 +175,7 @@
     moments = Moments(rel, v0)
     lanes_of = [slice(p * NZ, (p + 1) * NZ) for p in range(NP)]
     for x in range(CX):
-        moments.add(0, x, [cell_rows(v0, x, lanes_of[p]) for p in range(NP)])
+        moments.add(0, x, {p: cell_rows(v0, x, lanes_of[p]) for p in range(NP)})
 
     def first(plane):
         return (u0, plane - 3) if plane < 6 else (u0n, plane - 6)
@@ -183,31 +183,31 @@
     def scales_of(plane):
         return cell_rows(s, plane - 3, ALL) if plane < 6 else cell_rows(sn, plane - 6, ALL)
 
-    for plane in (4, 5, 6, 7):
-        scales, fields = scales_of(plane), []
-        for pair in range(NP // 2):
+    for pair in range(NP // 2):
+        for plane in (4, 5, 6, 7):
+            scales, fields = scales_of(plane), {}
             for q, g in enumerate(stencil(w_ref, [first(plane + d) for d in (-1, 0, 1)], pair)):
-                lanes = lanes_of[2 * pair + q]
-                v = [scales[y] * g[y] for y in range(NY)]
+                p = 2 * pair + q
+                lanes = lanes_of[p]
+                v = fields[p] = [scales[y] * g[y] for y in range(NY)]
                 store_scaled(u1_ref, slice((plane - 4) * PAD, (plane - 3) * PAD), lanes, scales, v)
-                fields.append(v)
                 if plane < 6:
                     for y in range(NY):
                         at = (plane - 4) * ROWS + y * PAD
                         v1_ref[at : at + PAD, lanes] = v[y]
-        if plane < 6:
-            moments.add(1, plane - 3, fields)
-    for plane in (5, 6):
-        scales, fields = scales_of(plane), []
-        for pair in range(NP // 2):
+            if plane < 6:
+                moments.add(1, plane - 3, fields)
+    for pair in range(NP // 2):
+        for plane in (5, 6):
+            scales, fields = scales_of(plane), {}
             for q, g in enumerate(stencil(w_ref, [(u1_ref, plane - 4 + d) for d in (-1, 0, 1)], pair)):
-                lanes = lanes_of[2 * pair + q]
+                p = 2 * pair + q
+                lanes = lanes_of[p]
                 before = cell_rows(v0, 2, lanes) if plane == 5 else cell_rows(v0n, 0, lanes)
-                v = [2.0 * (scales[y] * g[y]) - before[y] for y in range(NY)]
+                v = fields[p] = [2.0 * (scales[y] * g[y]) - before[y] for y in range(NY)]
                 store_scaled(u2_ref, slice((plane - 5) * PAD, (plane - 4) * PAD), lanes, scales, v)
-                fields.append(v)
-        if plane == 5:
-            moments.add(2, 2, fields)
+            if plane == 5:
+                moments.add(2, 2, fields)
     for n in range(4):
         for j in range(WIN):
             at = (n * WIN + j) * 8
@@ -235,33 +235,32 @@
 
     flat = out_ref.reshape(SIGN_ROWS, NZ)
     for step in range(3):
-        for plane in range(step + 1, step + 4):
+        for pair, plane in [(pair, plane) for pair in range(NP // 2) for plane in range(step + 1, step + 4)]:
             own = plane >= 3
             scales = cell_rows(s, plane - 3, ALL) if own else cell_rows(sf, plane, ALL)
-            fields = []
-            for pair in range(NP // 2):
-                planes = [source(step, plane + d) for d in (-1, 0, 1)]
-                for q, g in enumerate(stencil(w_ref, planes, pair)):
-                    p = 2 * pair + q
-                    lanes = lanes_of[p]
-                    v = [scales[y] * g[y] for y in range(NY)]
-                    if step == 1:
-                        before = cell_rows(v0, plane - 3, lanes) if own else cell_rows(v0f, plane, lanes)
-                        v = [2.0 * v[y] - before[y] for y in range(NY)]
-                    elif step == 2:
-                        before = cell_rows(v1f, 0, lanes) if plane == 3 else cell_rows(v1, plane - 4, lanes)
-                        v = [2.0 * v[y] - before[y] for y in range(NY)]
-                    if step == 0 and own:
-                        for y in range(NY):
-                            v1f[y * PAD : (y + 1) * PAD, lanes] = v[y]
-                    if step < 2:
-                        at = plane - 1 - step
-                        store_scaled((u1f, u2f)[step], slice(at * PAD, (at + 1) * PAD), lanes, scales, v)
-                    else:
-                        for y in range(NY):
-                            start = p * CELLS + turned(plane - 3) * NY + y
-                            flat[pl.ds(start, COMP, stride=NP * CELLS), :] = v[y][0:COMP]
-                    fields.append(v)
+            fields = {}
+            planes = [source(step, plane + d) for d in (-1, 0, 1)]
+            for q, g in enumerate(stencil(w_ref, planes, pair)):
+                p = 2 * pair + q
+                lanes = lanes_of[p]
+                v = [scales[y] * g[y] for y in range(NY)]
+                if step == 1:
+                    before = cell_rows(v0, plane - 3, lanes) if own else cell_rows(v0f, plane, lanes)
+                    v = [2.0 * v[y] - before[y] for y in range(NY)]
+                elif step == 2:
+                    before = cell_rows(v1f, 0, lanes) if plane == 3 else cell_rows(v1, plane - 4, lanes)
+                    v = [2.0 * v[y] - before[y] for y in range(NY)]
+                fields[p] = v
+                if step == 0 and own:
+                    for y in range(NY):
+                        v1f[y * PAD : (y + 1) * PAD, lanes] = v[y]
+                if step < 2:
+                    at = plane - 1 - step
+                    store_scaled((u1f, u2f)[step], slice(at * PAD, (at + 1) * PAD), lanes, scales, v)
+                else:
+                    for y in range(NY):
+                        start = p * CELLS + turned(plane - 3) * NY + y
+                        flat[pl.ds(start, COMP, stride=NP * CELLS), :] = v[y][0:COMP]
             if own:
                 moments.add(step + 1, plane - 3, fields)
 

time: 57.5 us -> 57.3 us (level)
  no operation moved by 1% of the time
where the time goes in v4:
time: 57.3 us; the launch traced here: 57 us
  blocking collectives  26.4 us (46%)
  starting transfers between devices  11.7 us (20%)
  waiting for transfers between devices  10.7 us (19%)
  Pallas kernels  5.52 us (10%)
  local copies, waits for them, and re-layouts  1.36 us (2%)
  between operations  0.7 us (1%)
  other arithmetic  0.65 us (1%)
    all_to_all x1, blocking collectives, body(): parts = lax.all_to_all(parts, NEAR, 0, 0, tiled=True).sum(0)  14.1 us
    all_to_all x1, blocking collectives, body(): near = lax.all_to_all(again, 'core', 0, 0, tiled=True)  12.3 us
    all_to_all x1, waiting for transfers between devices, body(): lax.all_to_all(parts, 'z', 0, 0, tiled=True).sum(0) * (1.0 / 368640)  10.7 us
    all_to_all x1, starting transfers between devices, body(): lax.all_to_all(parts, 'z', 0, 0, tiled=True).sum(0) * (1.0 / 368640)  6.74 us
    ppermute x1, starting transfers between devices, body(): lax.ppermute(payload, SPACE, [(i, (i + 1) % count if i % 2 else (i - 1) %...  4.94 us
    pallas_call x1, Pallas kernels, body(): pl.pallas_call(far_kernel, out_shape=(pltpu.VMEM((COMP * NP, CX, NY, NZ),...  1.82 us
    pallas_call x1, Pallas kernels, body(): pl.pallas_call(prepare_kernel, out_shape=(pltpu.VMEM((2, 2 * BAND, 2 * BA...  1.48 us
    pallas_call x1, Pallas kernels, body(): pl.pallas_call(near_kernel, out_shape=(pltpu.VMEM(HALF + (4 * PAD, WIDE),...  1.2 us
  transfers between devices with their start and end apart: 2, of which 1 were waited for; matrix products, arithmetic and copies ran while one was open for 1% of the time, Pallas kernels for 5%

profile of v4, /device:TPU:1, one launch (start us, length us, event | category | flops | bytes accessed | tf_op | source)
XLA Modules:
  0.0 57.0 jit_solution(7614127674444754414)
XLA Ops:
  0.6 1.0 %payload.1.own_ref = s32[784,128]{1,0:T(8,128)S(1)} custom-call(s32[360,2,128]{2,1,0:T(2,128)} %bitcast.8, s32[30,2,128]{2,1,0:T(2,128)} %bitcast.9), custom_call_target="tpu_custom_call" | custom-call | bytes 800000 | tf_op jit(solution)/shard_map/payload/pallas_call | solution.py:282
  1.6 0.0 copy-start
  1.7 4.9 %collective-permute-start = (s32[784,128]{1,0:T(8,128)S(1)}, s32[784,128]{1,0:T(8,128)S(1)}, u32[]{:S(2)}, u32[]{:S(2)}) collective-permute-start(s32[784,128]{1,0:T(8,128)S(1)} %payload.1.own_ref), channel_id=1, source_target_pairs={{0,504},{8,16},{16,8},{24,32},{32,24},{40,48},{48,40},{56,64},{64,... | collective-permute-start | bytes 1204232 | tf_op jit(solution)/shard_map/ppermute | solution.py:293
  6.6 0.0 copy-done
  6.6 1.5 %prepare.1 = (bf16[2,192,192]{2,1,0:T(8,128)(2,1)S(1)}, f32[8,128]{1,0:T(8,128)S(1)}, bf16[2,2,96,512]{3,2,1,0:T(8,128)(2,1)S(1)}, f32[192,512]{1,0:T(8,128)S(1)...) custom-call(f32[128]{0:T(128)} %mass_ref.1, f32[27,30,30]{2,1,0:T(8,128)} %fb_ref.1, ...), custom_call_target="tpu_custom_call" | custom-call | flops 1000000 | bytes 300000 | tf_op jit(solution)/shard_map/prepare/pallas_call | solution.py:295
  8.1 12.3 %all_to_all.21 = s32[2,784,128]{2,1,0:T(8,128)S(1)} all-to-all(s32[2,784,128]{2,1,0:T(8,128)S(1)} %bitcast.6), channel_id=1, replica_groups=mesh['xl'=2,'z'=16,'core'=2,'xh'=2,'y'=4] {'core'}, dimensions={0} | all-to-all | bytes 1605632 | tf_op jit(solution)/shard_map/all_to_all | solution.py:312
  20.4 1.2 %near_part.1 = (bf16[2,2,128,512]{3,2,1,0:T(8,128)(2,1)S(1)}, bf16[2,2,64,512]{3,2,1,0:T(8,128)(2,1)S(1)}, f32[128,512]{1,0:T(8,128)S(1)}, f32[128,128]{1,0:T(8,128)S(1)}) custom-call(s32[1568,128]{1,0:T(8,128)S(1)} %bitcast.7, bf16[2,192,192]{2,1,0:T(8,128)(2,1)S(1)} %get-tuple-element.15.w_ref, f32[8,128]{1,0:T(8,128)S(1)} %get-tuple-element.16.inv_ref, ...), custom_call_target="tpu_custom_call" | custom-call | flops 800000000 | bytes 1000000 | tf_op jit(solution)/shard_map/near_part/pallas_call | solution.py:314
  21.6 0.0 collective-permute-done.pay_ref
  21.6 1.8 %far_part.1 = (f32[120,3,2,128]{3,2,1,0:T(2,128)S(1)}, f32[32,4,128]{2,1,0:T(4,128)S(1)}) custom-call(s32[784,128]{1,0:T(8,128)S(1)} %collective-permute-done.pay_ref, bf16[2,192,192]{2,1,0:T(8,128)(2,1)S(1)} %get-tuple-element.15.w_ref, f32[8,128]{1,0:T(8,128)S(1)} %get-tuple-element.16.inv_ref, bf16[2,2,96,512]{3,2,1,0:T(8,128)(2,1)S(1)} %get-tuple-element.17.u0, ...), custom_call_target="tpu_custom_call" | custom-call | flops 1200000000 | bytes 2000000 | tf_op jit(solution)/shard_map/far_part/pallas_call | solution.py:335
  23.5 14.1 %all_to_all.22 = f32[32,4,128]{2,1,0:T(4,128)S(1)} all-to-all(f32[32,4,128]{2,1,0:T(4,128)S(1)} %get-tuple-element.26), channel_id=1, replica_groups=mesh['xl'=2,'z'=16,'core'=2,'xh'=2,'y'=4] {'xl','core','xh','y'}, dimensions={0} | all-to-all | bytes 131072 | tf_op jit(solution)/shard_map/all_to_all | solution.py:356
  37.6 0.6 %broadcast_in_dim.2 = f32[16,4,128]{2,1,0:T(4,128)} broadcast(f32[4,128]{1,0:T(4,128)S(1)} %reduce_sum.18), dimensions={1,2} | broadcast | bytes 34816 | tf_op jit(solution)/shard_map/broadcast_in_dim | solution.py:357
  38.2 6.7 %all-to-all-start.2 = ((f32[16,4,128]{2,1,0:T(4,128)}), f32[16,4,128]{2,1,0:T(4,128)S(1)}, u32[]{:S(2)}, u32[]{:S(2)}) async-start(f32[16,4,128]{2,1,0:T(4,128)} %broadcast_in_dim.2), calls=%async_computation.2 | async-start | bytes 65536 | tf_op jit(solution)/shard_map/all_to_all | solution.py:358
  44.9 0.7 %copy.8 = f32[30,4,3,2,128]{4,3,2,1,0:T(2,128)} copy(f32[30,4,3,2,128]{4,3,2,1,0:T(2,128)S(1)} %bitcast.5) | data formatting | bytes 737280
  45.7 10.7 %all-to-all-done.2 = f32[16,4,128]{2,1,0:T(4,128)S(1)} async-done(((f32[16,4,128]{2,1,0:T(4,128)}), f32[16,4,128]{2,1,0:T(4,128)S(1)}, u32[]{:S(2)}, u32[]{:S(2)}) %all-to-all-start.2) | async-done | bytes 32800 | tf_op jit(solution)/shard_map/all_to_all | solution.py:358
  56.4 0.6 %broadcast_multiply_fusion = f32[4,128]{1,0:T(4,128)} fusion(f32[4,128]{1,0:T(4,128)S(1)} %reduce_sum.19), kind=kLoop, calls=%fused_computation | loop fusion | flops 512 | bytes 4096 | tf_op jit(solution)/shard_map/mul | solution.py:358
  (2 shorter events, 0.1 us)
Async XLA Ops:
  1.6 5.0 %copy-start = (s32[784,128]{1,0:T(8,128)}, s32[784,128]{1,0:T(8,128)S(1)}, u32[]{:S(2)}) copy-start(s32[784,128]{1,0:T(8,128)S(1)} %payload.1.own_ref) | copy-start | bytes 1204228
  1.7 20.0 %collective-permute-start = (s32[784,128]{1,0:T(8,128)S(1)}, s32[784,128]{1,0:T(8,128)S(1)}, u32[]{:S(2)}, u32[]{:S(2)}) collective-permute-start(s32[784,128]{1,0:T(8,128)S(1)} %payload.1.own_ref), channel_id=1, source_target_pairs={{0,504},{8,16},{16,8},{24,32},{32,24},{40,48},{48,40},{56,64},{64,... | collective-permute-start | bytes 1204232 | tf_op jit(solution)/shard_map/ppermute | solution.py:293
  38.2 18.2 %all-to-all-start.2 = ((f32[16,4,128]{2,1,0:T(4,128)}), f32[16,4,128]{2,1,0:T(4,128)S(1)}, u32[]{:S(2)}, u32[]{:S(2)}) async-start(f32[16,4,128]{2,1,0:T(4,128)} %broadcast_in_dim.2), calls=%async_computation.2 | async-start | bytes 65536 | tf_op jit(solution)/shard_map/all_to_all | solution.py:358

commit v5 on v4

--- a/solution.py
+++ b/solution.py
@@ -331,7 +331,7 @@
         name="near_part",
     )(near, *prepared)
 
-    group = 32
+    group = lax.axis_size("z")
     last, parts = pl.pallas_call(
         far_kernel,
         out_shape=(
@@ -353,9 +353,9 @@
         name="far_part",
     )(far, *prepared, *shared)
 
-    parts = lax.all_to_all(parts, NEAR, 0, 0, tiled=True).sum(0)
-    parts = jnp.broadcast_to(parts[None], (lax.axis_size("z"), 4, NZ))
-    moments = lax.all_to_all(parts, "z", 0, 0, tiled=True).sum(0) * (1.0 / 368640)
+    parts = lax.all_to_all(parts, "z", 0, 0, tiled=True).sum(0)
+    parts = jnp.broadcast_to(parts[None], (32, 4, NZ))
+    moments = lax.all_to_all(parts, NEAR, 0, 0, tiled=True).sum(0) * (1.0 / 368640)
     return moments, last.reshape(COMP, NP, CX, NY, NZ)
 
 

time: 57.3 us -> 58.7 us (1.024)
  waiting for transfers between devices: 10.7 us -> 6.34 us
  blocking collectives: 26.4 us -> 29.3 us
  starting transfers between devices: 11.7 us -> 14.6 us
    all_to_all x1, waiting for transfers between devices: 10.7 us -> 6.33 us  [body(): lax.all_to_all(parts, NEAR, 0, 0, tiled=True).sum(0) * (1.0 / 368640)]
    all_to_all x1, blocking collectives: 14.1 us -> 17 us  [body(): parts = lax.all_to_all(parts, 'z', 0, 0, tiled=True).sum(0)]
    all_to_all x1, starting transfers between devices: 6.74 us -> 9.64 us  [body(): lax.all_to_all(parts, NEAR, 0, 0, tiled=True).sum(0) * (1.0 / 368640)]
where the time goes in v5:
time: 58.7 us; the launch traced here: 58.4 us
  blocking collectives  29.3 us (50%)
  starting transfers between devices  14.6 us (25%)
  waiting for transfers between devices  6.34 us (11%)
  Pallas kernels  5.51 us (9%)
  local copies, waits for them, and re-layouts  1.37 us (2%)
  between operations  0.7 us (1%)
  other arithmetic  0.65 us (1%)
    all_to_all x1, blocking collectives, body(): parts = lax.all_to_all(parts, 'z', 0, 0, tiled=True).sum(0)  17 us
    all_to_all x1, blocking collectives, body(): near = lax.all_to_all(again, 'core', 0, 0, tiled=True)  12.3 us
    all_to_all x1, starting transfers between devices, body(): lax.all_to_all(parts, NEAR, 0, 0, tiled=True).sum(0) * (1.0 / 368640)  9.64 us
    all_to_all x1, waiting for transfers between devices, body(): lax.all_to_all(parts, NEAR, 0, 0, tiled=True).sum(0) * (1.0 / 368640)  6.33 us
    ppermute x1, starting transfers between devices, body(): lax.ppermute(payload, SPACE, [(i, (i + 1) % count if i % 2 else (i - 1) %...  4.94 us
    pallas_call x1, Pallas kernels, body(): pl.pallas_call(far_kernel, out_shape=(pltpu.VMEM((COMP * NP, CX, NY, NZ),...  1.82 us
    pallas_call x1, Pallas kernels, body(): pl.pallas_call(prepare_kernel, out_shape=(pltpu.VMEM((2, 2 * BAND, 2 * BA...  1.48 us
    pallas_call x1, Pallas kernels, body(): pl.pallas_call(near_kernel, out_shape=(pltpu.VMEM(HALF + (4 * PAD, WIDE),...  1.2 us
  transfers between devices with their start and end apart: 2, of which 1 were waited for; matrix products, arithmetic and copies ran while one was open for 1% of the time, Pallas kernels for 5%

profile of v5, /device:TPU:1, one launch (start us, length us, event | category | flops | bytes accessed | tf_op | source)
XLA Modules:
  0.0 58.4 jit_solution(975648727453297008)
XLA Ops:
  0.6 1.0 %payload.1.own_ref = s32[784,128]{1,0:T(8,128)S(1)} custom-call(s32[360,2,128]{2,1,0:T(2,128)} %bitcast.8, s32[30,2,128]{2,1,0:T(2,128)} %bitcast.9), custom_call_target="tpu_custom_call" | custom-call | bytes 800000 | tf_op jit(solution)/shard_map/payload/pallas_call | solution.py:282
  1.6 0.0 copy-start
  1.7 4.9 %collective-permute-start = (s32[784,128]{1,0:T(8,128)S(1)}, s32[784,128]{1,0:T(8,128)S(1)}, u32[]{:S(2)}, u32[]{:S(2)}) collective-permute-start(s32[784,128]{1,0:T(8,128)S(1)} %payload.1.own_ref), channel_id=1, source_target_pairs={{0,504},{8,16},{16,8},{24,32},{32,24},{40,48},{48,40},{56,64},{64,... | collective-permute-start | bytes 1204232 | tf_op jit(solution)/shard_map/ppermute | solution.py:293
  6.6 0.0 copy-done
  6.6 1.5 %prepare.1 = (bf16[2,192,192]{2,1,0:T(8,128)(2,1)S(1)}, f32[8,128]{1,0:T(8,128)S(1)}, bf16[2,2,96,512]{3,2,1,0:T(8,128)(2,1)S(1)}, f32[192,512]{1,0:T(8,128)S(1)...) custom-call(f32[128]{0:T(128)} %mass_ref.1, f32[27,30,30]{2,1,0:T(8,128)} %fb_ref.1, ...), custom_call_target="tpu_custom_call" | custom-call | flops 1000000 | bytes 300000 | tf_op jit(solution)/shard_map/prepare/pallas_call | solution.py:295
  8.1 12.3 %all_to_all.21 = s32[2,784,128]{2,1,0:T(8,128)S(1)} all-to-all(s32[2,784,128]{2,1,0:T(8,128)S(1)} %bitcast.6), channel_id=1, replica_groups=mesh['xl'=2,'z'=16,'core'=2,'xh'=2,'y'=4] {'core'}, dimensions={0} | all-to-all | bytes 1605632 | tf_op jit(solution)/shard_map/all_to_all | solution.py:312
  20.4 1.2 %near_part.1 = (bf16[2,2,128,512]{3,2,1,0:T(8,128)(2,1)S(1)}, bf16[2,2,64,512]{3,2,1,0:T(8,128)(2,1)S(1)}, f32[128,512]{1,0:T(8,128)S(1)}, f32[128,128]{1,0:T(8,128)S(1)}) custom-call(s32[1568,128]{1,0:T(8,128)S(1)} %bitcast.7, bf16[2,192,192]{2,1,0:T(8,128)(2,1)S(1)} %get-tuple-element.15.w_ref, f32[8,128]{1,0:T(8,128)S(1)} %get-tuple-element.16.inv_ref, ...), custom_call_target="tpu_custom_call" | custom-call | flops 800000000 | bytes 1000000 | tf_op jit(solution)/shard_map/near_part/pallas_call | solution.py:314
  21.6 0.0 collective-permute-done.pay_ref
  21.6 1.8 %far_part.1 = (f32[120,3,2,128]{3,2,1,0:T(2,128)S(1)}, f32[16,4,128]{2,1,0:T(4,128)S(1)}) custom-call(s32[784,128]{1,0:T(8,128)S(1)} %collective-permute-done.pay_ref, bf16[2,192,192]{2,1,0:T(8,128)(2,1)S(1)} %get-tuple-element.15.w_ref, f32[8,128]{1,0:T(8,128)S(1)} %get-tuple-element.16.inv_ref, bf16[2,2,96,512]{3,2,1,0:T(8,128)(2,1)S(1)} %get-tuple-element.17.u0, ...), custom_call_target="tpu_custom_call" | custom-call | flops 1200000000 | bytes 2000000 | tf_op jit(solution)/shard_map/far_part/pallas_call | solution.py:335
  23.5 17.0 %all_to_all.22 = f32[16,4,128]{2,1,0:T(4,128)S(1)} all-to-all(f32[16,4,128]{2,1,0:T(4,128)S(1)} %get-tuple-element.26), channel_id=1, replica_groups=mesh['xl'=2,'z'=16,'core'=2,'xh'=2,'y'=4] {'z'}, dimensions={0} | all-to-all | bytes 65536 | tf_op jit(solution)/shard_map/all_to_all | solution.py:356
  40.5 0.6 %broadcast_in_dim.2 = f32[32,4,128]{2,1,0:T(4,128)} broadcast(f32[4,128]{1,0:T(4,128)S(1)} %reduce_sum.18), dimensions={1,2} | broadcast | bytes 67584 | tf_op jit(solution)/shard_map/broadcast_in_dim | solution.py:357
  41.1 9.6 %all-to-all-start.2 = ((f32[32,4,128]{2,1,0:T(4,128)}), f32[32,4,128]{2,1,0:T(4,128)S(1)}, u32[]{:S(2)}, u32[]{:S(2)}) async-start(f32[32,4,128]{2,1,0:T(4,128)} %broadcast_in_dim.2), calls=%async_computation.2 | async-start | bytes 131072 | tf_op jit(solution)/shard_map/all_to_all | solution.py:358
  50.7 0.7 %copy.8 = f32[30,4,3,2,128]{4,3,2,1,0:T(2,128)} copy(f32[30,4,3,2,128]{4,3,2,1,0:T(2,128)S(1)} %bitcast.5) | data formatting | bytes 737280
  51.5 6.3 %all-to-all-done.2 = f32[32,4,128]{2,1,0:T(4,128)S(1)} async-done(((f32[32,4,128]{2,1,0:T(4,128)}), f32[32,4,128]{2,1,0:T(4,128)S(1)}, u32[]{:S(2)}, u32[]{:S(2)}) %all-to-all-start.2) | async-done | bytes 65568 | tf_op jit(solution)/shard_map/all_to_all | solution.py:358
  57.8 0.6 broadcast_multiply_fusion
  (2 shorter events, 0.1 us)
Async XLA Ops:
  1.6 5.0 %copy-start = (s32[784,128]{1,0:T(8,128)}, s32[784,128]{1,0:T(8,128)S(1)}, u32[]{:S(2)}) copy-start(s32[784,128]{1,0:T(8,128)S(1)} %payload.1.own_ref) | copy-start | bytes 1204228
  1.7 20.0 %collective-permute-start = (s32[784,128]{1,0:T(8,128)S(1)}, s32[784,128]{1,0:T(8,128)S(1)}, u32[]{:S(2)}, u32[]{:S(2)}) collective-permute-start(s32[784,128]{1,0:T(8,128)S(1)} %payload.1.own_ref), channel_id=1, source_target_pairs={{0,504},{8,16},{16,8},{24,32},{32,24},{40,48},{48,40},{56,64},{64,... | collective-permute-start | bytes 1204232 | tf_op jit(solution)/shard_map/ppermute | solution.py:293
  41.1 16.7 %all-to-all-start.2 = ((f32[32,4,128]{2,1,0:T(4,128)}), f32[32,4,128]{2,1,0:T(4,128)S(1)}, u32[]{:S(2)}, u32[]{:S(2)}) async-start(f32[32,4,128]{2,1,0:T(4,128)} %broadcast_in_dim.2), calls=%async_computation.2 | async-start | bytes 131072 | tf_op jit(solution)/shard_map/all_to_all | solution.py:358

commit v6 on v4

--- a/solution.py
+++ b/solution.py
@@ -215,7 +215,7 @@
 
 
 def far_kernel(
-    pay_ref, w_ref, inv_ref, u0, v0, s, rel, u1, u2, v1, sums_ref, out_ref, pm_ref, u0f, v0f, sf, u1f, u2f, v1f
+    pay_ref, w_ref, inv_ref, u0, v0, s, rel, u1, u2, v1, sums_ref, out_ref, pm_ref, u0f, v0f, sf, u1f, u2f, v1f, result, sems
 ):
     inv = [inv_ref[j : j + 1, :] for j in range(WIN)]
     load_slab(pay_ref, window_of(neighbour(0)), inv, u0f, v0f, sf)
@@ -233,7 +233,7 @@
             return (u1f, plane - 1) if plane < 4 else (u1, plane - 4)
         return (u2f, plane - 2) if plane < 5 else (u2, plane - 5)
 
-    flat = out_ref.reshape(SIGN_ROWS, NZ)
+    writes = []
     for step in range(3):
         for pair, plane in [(pair, plane) for pair in range(NP // 2) for plane in range(step + 1, step + 4)]:
             own = plane >= 3
@@ -259,8 +259,14 @@
                     store_scaled((u1f, u2f)[step], slice(at * PAD, (at + 1) * PAD), lanes, scales, v)
                 else:
                     for y in range(NY):
-                        start = p * CELLS + turned(plane - 3) * NY + y
-                        flat[pl.ds(start, COMP, stride=NP * CELLS), :] = v[y][0:COMP]
+                        result[plane - 3, pl.ds(p * NY + y, COMP, stride=NP * NY), :] = v[y][0:COMP]
+            if step == 2 and pair == NP // 2 - 1:
+                x = plane - 3
+                write = pltpu.make_async_copy(
+                    result.at[x].reshape(COMP * NP, NY, NZ), out_ref.at[:, turned(x)], sems.at[x]
+                )
+                write.start()
+                writes.append(write)
             if own:
                 moments.add(step + 1, plane - 3, fields)
 
@@ -271,6 +277,8 @@
         value = jnp.sum(stacked, axis=1, keepdims=True)
         total = total + jnp.where(lane == ((window_of(own_index()) + j) & 127), value, 0.0)
     pm_ref[...] = jnp.broadcast_to(total[None], pm_ref.shape)
+    for write in writes:
+        write.wait()
 
 
 HBM = pl.BlockSpec(memory_space=pltpu.HBM)
@@ -335,11 +343,11 @@
     last, parts = pl.pallas_call(
         far_kernel,
         out_shape=(
-            pltpu.VMEM((COMP * NP, CX, NY, NZ), jnp.float32),
+            jax.ShapeDtypeStruct((COMP * NP, CX, NY, NZ), jnp.float32),
             pltpu.VMEM((group, 4, NZ), jnp.float32),
         ),
         in_specs=[VMEM] * 11,
-        out_specs=(VMEM, VMEM),
+        out_specs=(HBM, VMEM),
         scratch_shapes=[
             pltpu.VMEM(slab, jnp.bfloat16),
             pltpu.VMEM((CX * ROWS, WIDE), jnp.float32),
@@ -347,6 +355,8 @@
             pltpu.VMEM(slab, jnp.bfloat16),
             pltpu.VMEM(slab, jnp.bfloat16),
             pltpu.VMEM((ROWS, WIDE), jnp.float32),
+            pltpu.VMEM((CX, SIGN_ROWS // CX, NZ), jnp.float32),
+            pltpu.SemaphoreType.DMA((CX,)),
         ],
         compiler_params=pltpu.CompilerParams(vmem_limit_bytes=24 * 2**20),
         cost_estimate=pl.CostEstimate(flops=1200000000, bytes_accessed=2000000, transcendentals=0),

time: 57.3 us -> 57.1 us (level)
  blocking collectives: 26.4 us -> 44.4 us
  waiting for transfers between devices: 10.7 us -> 0.01 us
  starting transfers between devices: 11.7 us -> 4.94 us
  local copies, waits for them, and re-layouts: 1.36 us -> 0.01 us
  Pallas kernels: 5.52 us -> 6.11 us
    all_to_all x0 -> x1, blocking collectives: none -> 18 us  [body(): lax.all_to_all(parts, 'z', 0, 0, tiled=True).sum(0) * (1.0 / 368640)]
    all_to_all x1 -> x0, waiting for transfers between devices: 10.7 us -> none  [body(): lax.all_to_all(parts, 'z', 0, 0, tiled=True).sum(0) * (1.0 / 368640)]
    all_to_all x1 -> x0, starting transfers between devices: 6.74 us -> none  [body(): lax.all_to_all(parts, 'z', 0, 0, tiled=True).sum(0) * (1.0 / 368640)]
    unnamed x3 -> x2, local copies, waits for them, and re-layouts: 0.74 us -> 0.01 us
    broadcast_in_dim x1, local copies, waits for them, and re-layouts: 0.61 us -> 0.01 us  [body(): parts = jnp.broadcast_to(parts[None], (lax.axis_size('z'), 4, NZ))]
    pallas_call x1, Pallas kernels: 1.82 us -> 2.42 us  [body(): pl.pallas_call(far_kernel, out_shape=(jax.ShapeDtypeStruct((COMP * NP, CX...]
  transfers between devices with their start and end apart: 2 -> 1, of which waited for: 1 -> 0; matrix products, arithmetic and copies ran while one was open for 1% -> 0% of each run, Pallas kernels for 5% -> 5%
where the time goes in v6:
time: 57.1 us; the launch traced here: 56.8 us
  blocking collectives  44.4 us (78%)
  Pallas kernels  6.11 us (11%)
  starting transfers between devices  4.94 us (9%)
  between operations  0.7 us (1%)
  other arithmetic  0.65 us (1%)
    all_to_all x1, blocking collectives, body(): lax.all_to_all(parts, 'z', 0, 0, tiled=True).sum(0) * (1.0 / 368640)  18 us
    all_to_all x1, blocking collectives, body(): parts = lax.all_to_all(parts, NEAR, 0, 0, tiled=True).sum(0)  14.1 us
    all_to_all x1, blocking collectives, body(): near = lax.all_to_all(again, 'core', 0, 0, tiled=True)  12.3 us
    ppermute x1, starting transfers between devices, body(): lax.ppermute(payload, SPACE, [(i, (i + 1) % count if i % 2 else (i - 1) %...  4.94 us
    pallas_call x1, Pallas kernels, body(): pl.pallas_call(far_kernel, out_shape=(jax.ShapeDtypeStruct((COMP * NP, CX...  2.42 us
    pallas_call x1, Pallas kernels, body(): pl.pallas_call(prepare_kernel, out_shape=(pltpu.VMEM((2, 2 * BAND, 2 * BA...  1.48 us
    pallas_call x1, Pallas kernels, body(): pl.pallas_call(near_kernel, out_shape=(pltpu.VMEM(HALF + (4 * PAD, WIDE),...  1.2 us
  transfers between devices with their start and end apart: 1, of which 0 were waited for; matrix products, arithmetic and copies ran while one was open for 0% of the time, Pallas kernels for 5%

profile of v6, /device:TPU:1, one launch (start us, length us, event | category | flops | bytes accessed | tf_op | source)
XLA Modules:
  0.0 56.8 jit_solution(6680968729920087707)
XLA Ops:
  0.6 1.0 %payload.1.own_ref = s32[784,128]{1,0:T(8,128)S(1)} custom-call(s32[360,2,128]{2,1,0:T(2,128)} %bitcast.7, s32[30,2,128]{2,1,0:T(2,128)} %bitcast.8), custom_call_target="tpu_custom_call" | custom-call | bytes 800000 | tf_op jit(solution)/shard_map/payload/pallas_call | solution.py:290
  1.6 0.0 copy-start
  1.7 4.9 %collective-permute-start = (s32[784,128]{1,0:T(8,128)S(1)}, s32[784,128]{1,0:T(8,128)S(1)}, u32[]{:S(2)}, u32[]{:S(2)}) collective-permute-start(s32[784,128]{1,0:T(8,128)S(1)} %payload.1.own_ref), channel_id=1, source_target_pairs={{0,504},{8,16},{16,8},{24,32},{32,24},{40,48},{48,40},{56,64},{64,... | collective-permute-start | bytes 1204232 | tf_op jit(solution)/shard_map/ppermute | solution.py:301
  6.6 0.0 copy-done
  6.6 1.5 %prepare.1 = (bf16[2,192,192]{2,1,0:T(8,128)(2,1)S(1)}, f32[8,128]{1,0:T(8,128)S(1)}, bf16[2,2,96,512]{3,2,1,0:T(8,128)(2,1)S(1)}, f32[192,512]{1,0:T(8,128)S(1)...) custom-call(f32[128]{0:T(128)} %mass_ref.1, f32[27,30,30]{2,1,0:T(8,128)} %fb_ref.1, ...), custom_call_target="tpu_custom_call" | custom-call | flops 1000000 | bytes 300000 | tf_op jit(solution)/shard_map/prepare/pallas_call | solution.py:303
  8.1 12.3 %all_to_all.21 = s32[2,784,128]{2,1,0:T(8,128)S(1)} all-to-all(s32[2,784,128]{2,1,0:T(8,128)S(1)} %bitcast.5), channel_id=1, replica_groups=mesh['xl'=2,'z'=16,'core'=2,'xh'=2,'y'=4] {'core'}, dimensions={0} | all-to-all | bytes 1605632 | tf_op jit(solution)/shard_map/all_to_all | solution.py:320
  20.4 1.2 %near_part.1 = (bf16[2,2,128,512]{3,2,1,0:T(8,128)(2,1)S(1)}, bf16[2,2,64,512]{3,2,1,0:T(8,128)(2,1)S(1)}, f32[128,512]{1,0:T(8,128)S(1)}, f32[128,128]{1,0:T(8,128)S(1)}) custom-call(s32[1568,128]{1,0:T(8,128)S(1)} %bitcast.6, bf16[2,192,192]{2,1,0:T(8,128)(2,1)S(1)} %get-tuple-element.15.w_ref, f32[8,128]{1,0:T(8,128)S(1)} %get-tuple-element.16.inv_ref, ...), custom_call_target="tpu_custom_call" | custom-call | flops 800000000 | bytes 1000000 | tf_op jit(solution)/shard_map/near_part/pallas_call | solution.py:322
  21.6 0.0 collective-permute-done.pay_ref
  21.6 2.4 %far_part.1 = (f32[120,3,2,128]{3,2,1,0:T(2,128)}, f32[32,4,128]{2,1,0:T(4,128)S(1)}) custom-call(s32[784,128]{1,0:T(8,128)S(1)} %collective-permute-done.pay_ref, bf16[2,192,192]{2,1,0:T(8,128)(2,1)S(1)} %get-tuple-element.15.w_ref, f32[8,128]{1,0:T(8,128)S(1)} %get-tuple-element.16.inv_ref, bf16[2,2,96,512]{3,2,1,0:T(8,128)(2,1)S(1)} %get-tuple-element.17.u0, ...), custom_call_target="tpu_custom_call" | custom-call | flops 1200000000 | bytes 2000000 | tf_op jit(solution)/shard_map/far_part/pallas_call | solution.py:343
  24.1 14.1 %all_to_all.22 = f32[32,4,128]{2,1,0:T(4,128)S(1)} all-to-all(f32[32,4,128]{2,1,0:T(4,128)S(1)} %get-tuple-element.26), channel_id=1, replica_groups=mesh['xl'=2,'z'=16,'core'=2,'xh'=2,'y'=4] {'xl','core','xh','y'}, dimensions={0} | all-to-all | bytes 131072 | tf_op jit(solution)/shard_map/all_to_all | solution.py:366
  38.2 18.0 %all_to_all.23 = f32[16,4,128]{2,1,0:T(4,128)S(1)} all-to-all(f32[16,4,128]{2,1,0:T(4,128)S(1)} %broadcast_in_dim.2), channel_id=1, replica_groups=mesh['xl'=2,'z'=16,'core'=2,'xh'=2,'y'=4] {'z'}, dimensions={0} | all-to-all | bytes 65536 | tf_op jit(solution)/shard_map/all_to_all | solution.py:368
  56.2 0.6 %broadcast_multiply_fusion = f32[4,128]{1,0:T(4,128)} fusion(f32[4,128]{1,0:T(4,128)S(1)} %reduce_sum.19), kind=kLoop, calls=%fused_computation | loop fusion | flops 512 | bytes 4096 | tf_op jit(solution)/shard_map/mul | solution.py:368
  (3 shorter events, 0.1 us)
Async XLA Ops:
  1.6 5.0 %copy-start = (s32[784,128]{1,0:T(8,128)}, s32[784,128]{1,0:T(8,128)S(1)}, u32[]{:S(2)}) copy-start(s32[784,128]{1,0:T(8,128)S(1)} %payload.1.own_ref) | copy-start | bytes 1204228
  1.7 20.0 %collective-permute-start = (s32[784,128]{1,0:T(8,128)S(1)}, s32[784,128]{1,0:T(8,128)S(1)}, u32[]{:S(2)}, u32[]{:S(2)}) collective-permute-start(s32[784,128]{1,0:T(8,128)S(1)} %payload.1.own_ref), channel_id=1, source_target_pairs={{0,504},{8,16},{16,8},{24,32},{32,24},{40,48},{48,40},{56,64},{64,... | collective-permute-start | bytes 1204232 | tf_op jit(solution)/shard_map/ppermute | solution.py:301
